TPU v7x, 32 devices: a whole 2x2x4 slice. The times are simulated.
32 devices in a mesh: hour: 4 (over y, core), lat: 2 (over x), lon: 4 (over z).
Axes of the slice: x: 2, y: 2, z: 4, core: 2. Of those that a mesh axis runs over, the one named last changes fastest.
Arguments:
- precip: float32 [4, 1024, 2048], P('hour', 'lat', 'lon'), may hold values from 0.05 to 5
- scaling: float32 [4, 1024, 2048], P('hour', 'lat', 'lon'), may hold values from 0.5 to 2
- hour_weight: float32 [4], P('hour'), may hold values from 0.03 to 0.3
- cotangent: float32 [4, 1024, 2048], P('hour', 'lat', 'lon'), may hold values from -6 to 6
Outputs:
- grad_precip: float32 [4, 1024, 2048], P('hour', 'lat', 'lon')
- grad_scaling: float32 [4, 1024, 2048], P('hour', 'lat', 'lon')
All inputs are finite; a program needn't handle non-finite values.
Results may differ from a plain program's by a relative error of at most 0.00012.
Values sent between devices are 32-bit elements; how exact they have to be, the bound alone decides.
A program may use at most 64 MiB of HBM per device.

v0:
```python
import jax
import jax.numpy as jnp
from jax import lax
from jax.sharding import PartitionSpec as P

RADIUS = 8


PHI = 0.8
SPREAD = 50.0


def with_halo(block, sides, width, periodic):
    for axis, dim in sides:
        count = lax.axis_size(axis)
        forward = [(i, i + 1) for i in range(count - 1)]
        if periodic:
            forward.append((count - 1, 0))
        backward = [(target, source) for source, target in forward]
        low = lax.ppermute(
            lax.slice_in_dim(block, block.shape[dim] - width, None, axis=dim), axis, forward
        )
        high = lax.ppermute(lax.slice_in_dim(block, 0, width, axis=dim), axis, backward)
        block = jnp.concatenate([low, block, high], axis=dim)
    return block


def band_matrix(size):
    offsets = jnp.arange(-RADIUS, RADIUS + 1).astype(jnp.float32)
    total = jnp.sum(jnp.exp(-offsets * offsets / SPREAD))
    outer = lax.broadcasted_iota(jnp.int32, (size, size + 2 * RADIUS), 0)
    inner = lax.broadcasted_iota(jnp.int32, (size, size + 2 * RADIUS), 1)
    spacing = (inner - outer - RADIUS).astype(jnp.float32)
    inside = jnp.abs(inner - outer - RADIUS) <= RADIUS
    return jnp.where(inside, jnp.exp(-spacing * spacing / SPREAD) / total, 0.0)


def pass_rows(padded, count):
    pieces = []
    for start in range(0, count, 256):
        size = min(256, count - start)
        pieces.append(
            jnp.dot(
                band_matrix(size),
                padded[start : start + size + 2 * RADIUS],
                precision=lax.Precision.HIGHEST,
            )
        )
    return jnp.concatenate(pieces, axis=0)


def pass_cols(padded, count):
    pieces = []
    for start in range(0, count, 256):
        size = min(256, count - start)
        pieces.append(
            jnp.dot(
                padded[:, start : start + size + 2 * RADIUS],
                band_matrix(size).T,
                precision=lax.Precision.HIGHEST,
            )
        )
    return jnp.concatenate(pieces, axis=1)


def smooth(field):
    rows, cols = field.shape
    tall = with_halo(field, (("lat", 0),), RADIUS, False)
    full = with_halo(tall, (("lon", 1),), RADIUS, True)
    return pass_cols(pass_rows(full, rows), cols)


def per_device(precip, scaling, hour_weight, cotangent):
    rainfall = precip[0]
    incoming = scaling[0]
    upstream = cotangent[0]
    weight = hour_weight[0]
    first = smooth(incoming)
    lifted = jnp.power(rainfall / first, PHI)
    second = smooth(lifted)
    logb = jnp.log(second)
    logq, pooled = lax.psum((weight * logb, upstream * jnp.exp(-PHI * logb)), "hour")
    terms = PHI * upstream * jnp.exp(PHI * (logq - logb))
    dlogq = PHI * jnp.exp(PHI * logq) * pooled
    dsecond = (weight * dlogq - terms) / second
    dlifted = smooth(dsecond)
    carried = PHI * dlifted * lifted
    grad_precip = carried / rainfall
    grad_scaling = smooth(-carried / first)
    return (grad_precip[None], grad_scaling[None])


def solution(mesh):
    in_specs = (
        P("hour", "lat", "lon"),
        P("hour", "lat", "lon"),
        P("hour"),
        P("hour", "lat", "lon"),
    )
    out_specs = (P("hour", "lat", "lon"), P("hour", "lat", "lon"))
    return jax.shard_map(
        per_device, mesh=mesh, in_specs=in_specs, out_specs=out_specs, check_vma=False
    )
```

profile of v0, /device:TPU:0, one launch (start us, length us, event | category | flops | bytes accessed | tf_op | source)
XLA Modules:
  0.0 185.5 jit_solution(14626654992111271097)
XLA Ops:
  8.0 4.8 %collective-permute-start = (f32[8,512]{1,0:T(8,128)S(1)}, f32[8,512]{1,0:T(8,128)S(1)}, u32[]{:S(2)}, u32[]{:S(2)}) collective-permute-start(f32[8,512]{1,0:T(8,128)S(1)} %get-tuple-element.22), channel_id=1, source_target_pairs={{0,4},{1,5},{2,6},{3,7},{8,12},{9,13},{10,14},{11,15},{16,20},{17,... | collective-permute-start | bytes 49160 | tf_op jit(solution)/shard_map/ppermute | solution.py:20
  14.3 4.2 %collective-permute-done.1 = f32[8,512]{1,0:T(8,128)S(1)} collective-permute-done((f32[8,512]{1,0:T(8,128)S(1)}, f32[8,512]{1,0:T(8,128)S(1)}, u32[]{:S(2)}, u32[]{:S(2)}) %collective-permute-start.1) | collective-permute-done | bytes 16416 | tf_op jit(solution)/shard_map/ppermute | solution.py:23
  18.5 1.9 %pad_maximum_fusion.16 = (f32[528,8]{1,0:T(8,128)}, f32[528,8]{1,0:T(8,128)}) fusion(f32[8,512]{1,0:T(8,128)S(1)} %collective-permute-done.1, f32[512,512]{1,0:T(8,128)} %bitcast.31, f32[8,512]{1,0:T(8,128)S(1)} %collective-permute-done), kind=kLoop, calls=%fused_computation.76 | loop fusion | flops 16896 | bytes 1115136 | tf_op jit(solution)/shard_map/slice | solution.py:21
  22.0 2.2 %collective-permute-start.3 = (f32[528,8]{1,0:T(8,128)}, f32[528,8]{1,0:T(8,128)}, u32[]{:S(2)}, u32[]{:S(2)}) collective-permute-start(f32[528,8]{1,0:T(8,128)} %get-tuple-element.13), channel_id=1, source_target_pairs={{1,0},{2,1},{3,2},{0,3},{5,4},{6,5},{7,6},{4,7},{9,8},{10,9},{11,1... | collective-permute-start | bytes 50696 | tf_op jit(solution)/shard_map/ppermute | solution.py:23
  25.3 6.6 %collective-permute-done.2 = f32[528,8]{1,0:T(8,128)S(1)} collective-permute-done((f32[528,8]{1,0:T(8,128)}, f32[528,8]{1,0:T(8,128)S(1)}, u32[]{:S(2)}, u32[]{:S(2)}) %collective-permute-start.2) | collective-permute-done | bytes 16928 | tf_op jit(solution)/shard_map/ppermute | solution.py:20
  31.8 2.8 %collective-permute-done.3 = f32[528,8]{1,0:T(8,128)} collective-permute-done((f32[528,8]{1,0:T(8,128)}, f32[528,8]{1,0:T(8,128)}, u32[]{:S(2)}, u32[]{:S(2)}) %collective-permute-start.3) | collective-permute-done | bytes 16928 | tf_op jit(solution)/shard_map/ppermute | solution.py:23
  36.1 2.3 %fusion.22 = f32[256,528]{0,1:T(8,128)S(1)} fusion(f32[528,528]{1,0:T(8,128)S(1)} %pad_maximum_fusion, f32[]{:T(128)} %fusion.68), kind=kOutput, calls=%fused_computation.44 | convolution fusion | flops 441884672 | bytes 1236996 | tf_op jit(solution)/shard_map/dot_general | solution.py:43
  38.3 2.3 %fusion.24 = f32[256,528]{0,1:T(8,128)S(1)} fusion(f32[528,528]{1,0:T(8,128)S(1)} %pad_maximum_fusion, f32[]{:T(128)} %fusion.68), kind=kOutput, calls=%fused_computation.46 | convolution fusion | flops 441884672 | bytes 1236996 | tf_op jit(solution)/shard_map/dot_general | solution.py:43
  45.1 1.9 %collective-permute-start.4 = (f32[8,512]{0,1:T(8,128)S(1)}, f32[8,512]{0,1:T(8,128)S(1)}, u32[]{:S(2)}, u32[]{:S(2)}) collective-permute-start(f32[8,512]{0,1:T(8,128)S(1)} %get-tuple-element.20), channel_id=1, source_target_pairs={{0,4},{1,5},{2,6},{3,7},{8,12},{9,13},{10,14},{11,15},{16,20},{17,... | collective-permute-start | bytes 49160 | tf_op jit(solution)/shard_map/ppermute | solution.py:20
  48.3 3.7 %collective-permute-done.4 = f32[8,512]{0,1:T(8,128)S(1)} collective-permute-done((f32[8,512]{0,1:T(8,128)S(1)}, f32[8,512]{0,1:T(8,128)S(1)}, u32[]{:S(2)}, u32[]{:S(2)}) %collective-permute-start.4) | collective-permute-done | bytes 16416 | tf_op jit(solution)/shard_map/ppermute | solution.py:20
  52.1 4.1 %collective-permute-done.5 = f32[8,512]{0,1:T(8,128)S(1)} collective-permute-done((f32[8,512]{0,1:T(8,128)S(1)}, f32[8,512]{0,1:T(8,128)S(1)}, u32[]{:S(2)}, u32[]{:S(2)}) %collective-permute-start.5) | collective-permute-done | bytes 16416 | tf_op jit(solution)/shard_map/ppermute | solution.py:23
  56.3 1.8 collective-permute-start.6
  58.1 2.0 %collective-permute-start.7 = (f32[528,8]{0,1:T(8,128)S(1)}, f32[528,8]{0,1:T(8,128)S(1)}, u32[]{:S(2)}, u32[]{:S(2)}) collective-permute-start(f32[528,8]{0,1:T(8,128)S(1)} %get-tuple-element.11), channel_id=1, source_target_pairs={{1,0},{2,1},{3,2},{0,3},{5,4},{6,5},{7,6},{4,7},{9,8},{10,9},{11,1... | collective-permute-start | bytes 50696 | tf_op jit(solution)/shard_map/ppermute | solution.py:23
  63.8 1.8 fusion.18
  65.5 1.8 fusion.20
  72.5 51.8 %all-reduce.3.cloned.1.call-done = (f32[512,512]{0,1:T(8,128)}, f32[512,512]{0,1:T(8,128)}) async-done(((f32[512,512]{0,1:T(8,128)}, f32[512,512]{0,1:T(8,128)}), (f32[512,512]{0,1:T(8,128)}, f32[512,512]{0,1:T(8,128)})) %all-reduce.3.cloned.1.call-update) | async-done | bytes 2097168 | tf_op jit(solution)/shard_map/psum | solution.py:82
  124.3 2.1 %fusion.8 = f32[512,512]{0,1:T(8,128)S(1)} fusion(f32[1,512,512]{1,2,0:T(8,128)S(1)} %copy.7, f32[512,512]{0,1:T(8,128)} %get-tuple-element.4, f32[512,512]{0,1:T(8,128)} %get-tuple-element.5, f32[512,256]{0,1:T(8,128)S(1)} %fusion.42, f32[512,256]{0,1:T(8,128)S(1)} %fusion.33, f32[]{:T(128)} %bitcast.28), kind=kLoop, calls=%fused_computation.28 | loop fusion | flops 2883584 | bytes 5242884 | tf_op jit(solution)/shard_map/div | solution.py:85
  126.6 3.4 %collective-permute-start.8 = (f32[8,512]{0,1:T(8,128)S(1)}, f32[8,512]{0,1:T(8,128)S(1)}, u32[]{:S(2)}, u32[]{:S(2)}) collective-permute-start(f32[8,512]{0,1:T(8,128)S(1)} %get-tuple-element.16), channel_id=1, source_target_pairs={{0,4},{1,5},{2,6},{3,7},{8,12},{9,13},{10,14},{11,15},{16,20},{17,... | collective-permute-start | bytes 49160 | tf_op jit(solution)/shard_map/ppermute | solution.py:20
  131.3 4.2 %collective-permute-done.8 = f32[8,512]{0,1:T(8,128)S(1)} collective-permute-done((f32[8,512]{0,1:T(8,128)S(1)}, f32[8,512]{0,1:T(8,128)S(1)}, u32[]{:S(2)}, u32[]{:S(2)}) %collective-permute-start.8) | collective-permute-done | bytes 16416 | tf_op jit(solution)/shard_map/ppermute | solution.py:20
  135.4 4.1 %collective-permute-done.9 = f32[8,512]{0,1:T(8,128)S(1)} collective-permute-done((f32[8,512]{0,1:T(8,128)S(1)}, f32[8,512]{0,1:T(8,128)S(1)}, u32[]{:S(2)}, u32[]{:S(2)}) %collective-permute-start.9) | collective-permute-done | bytes 16416 | tf_op jit(solution)/shard_map/ppermute | solution.py:23
  141.1 2.3 %collective-permute-start.11 = (f32[528,8]{0,1:T(8,128)S(1)}, f32[528,8]{0,1:T(8,128)S(1)}, u32[]{:S(2)}, u32[]{:S(2)}) collective-permute-start(f32[528,8]{0,1:T(8,128)S(1)} %get-tuple-element.9), channel_id=1, source_target_pairs={{1,0},{2,1},{3,2},{0,3},{5,4},{6,5},{7,6},{4,7},{9,8},{10,9},{11,1... | collective-permute-start | bytes 50696 | tf_op jit(solution)/shard_map/ppermute | solution.py:23
  143.5 1.8 collective-permute-done.10
  145.7 1.8 fusion.14
  147.5 1.8 fusion.16
  151.0 1.8 fusion.30
  156.7 2.6 %collective-permute-done.12 = f32[8,512]{0,1:T(8,128)S(1)} collective-permute-done((f32[8,512]{0,1:T(8,128)S(1)}, f32[8,512]{0,1:T(8,128)S(1)}, u32[]{:S(2)}, u32[]{:S(2)}) %collective-permute-start.12) | collective-permute-done | bytes 16416 | tf_op jit(solution)/shard_map/ppermute | solution.py:20
  159.3 4.4 %collective-permute-done.13 = f32[8,512]{0,1:T(8,128)S(1)} collective-permute-done((f32[8,512]{0,1:T(8,128)S(1)}, f32[8,512]{0,1:T(8,128)S(1)}, u32[]{:S(2)}, u32[]{:S(2)}) %collective-permute-start.13) | collective-permute-done | bytes 16416 | tf_op jit(solution)/shard_map/ppermute | solution.py:23
  164.9 2.7 %collective-permute-start.15 = (f32[528,8]{0,1:T(8,128)S(1)}, f32[528,8]{0,1:T(8,128)S(1)}, u32[]{:S(2)}, u32[]{:S(2)}) collective-permute-start(f32[528,8]{0,1:T(8,128)S(1)} %get-tuple-element.7), channel_id=1, source_target_pairs={{1,0},{2,1},{3,2},{0,3},{5,4},{6,5},{7,6},{4,7},{9,8},{10,9},{11,1... | collective-permute-start | bytes 50696 | tf_op jit(solution)/shard_map/ppermute | solution.py:23
  170.2 1.8 fusion.10
  172.0 1.8 fusion.12
  173.8 1.7 fusion.38
  175.5 1.7 fusion.27
  (60 shorter events, 34.5 us)
Async XLA Ops:
  7.2 17.1 %copy-start.8 = (f32[1,512,512]{2,1,0:T(8,128)S(1)}, f32[1,512,512]{2,1,0:T(8,128)}, u32[]{:S(2)}) copy-start(f32[1,512,512]{2,1,0:T(8,128)} %param.4) | copy-start | bytes 3145732
  7.2 117.1 %all-reduce.3.cloned.1.call-start = ((), (), s32[]{:S(2)}) async-start(), calls=%async_computation | async-start | bytes 4194304 | tf_op jit(solution)/shard_map/psum | solution.py:82
  8.0 6.3 %collective-permute-start = (f32[8,512]{1,0:T(8,128)S(1)}, f32[8,512]{1,0:T(8,128)S(1)}, u32[]{:S(2)}, u32[]{:S(2)}) collective-permute-start(f32[8,512]{1,0:T(8,128)S(1)} %get-tuple-element.22), channel_id=1, source_target_pairs={{0,4},{1,5},{2,6},{3,7},{8,12},{9,13},{10,14},{11,15},{16,20},{17,... | collective-permute-start | bytes 49160 | tf_op jit(solution)/shard_map/ppermute | solution.py:20
  12.9 5.6 %collective-permute-start.1 = (f32[8,512]{1,0:T(8,128)S(1)}, f32[8,512]{1,0:T(8,128)S(1)}, u32[]{:S(2)}, u32[]{:S(2)}) collective-permute-start(f32[8,512]{1,0:T(8,128)S(1)} %get-tuple-element.23), channel_id=1, source_target_pairs={{4,0},{5,1},{6,2},{7,3},{12,8},{13,9},{14,10},{15,11},{20,16},{21,... | collective-permute-start | bytes 49160 | tf_op jit(solution)/shard_map/ppermute | solution.py:23
  20.4 14.2 %copy-start.4 = (f32[1,512,512]{2,1,0:T(8,128)S(1)}, f32[1,512,512]{2,1,0:T(8,128)}, u32[]{:S(2)}) copy-start(f32[1,512,512]{2,1,0:T(8,128)} %param.5) | copy-start | bytes 3145732
  20.4 11.4 %collective-permute-start.2 = (f32[528,8]{1,0:T(8,128)}, f32[528,8]{1,0:T(8,128)S(1)}, u32[]{:S(2)}, u32[]{:S(2)}) collective-permute-start(f32[528,8]{1,0:T(8,128)} %get-tuple-element.12), channel_id=1, source_target_pairs={{0,1},{1,2},{2,3},{3,0},{4,5},{5,6},{6,7},{7,4},{8,9},{9,10},{10,1... | collective-permute-start | bytes 50696 | tf_op jit(solution)/shard_map/ppermute | solution.py:20
  22.0 12.6 %collective-permute-start.3 = (f32[528,8]{1,0:T(8,128)}, f32[528,8]{1,0:T(8,128)}, u32[]{:S(2)}, u32[]{:S(2)}) collective-permute-start(f32[528,8]{1,0:T(8,128)} %get-tuple-element.13), channel_id=1, source_target_pairs={{1,0},{2,1},{3,2},{0,3},{5,4},{6,5},{7,6},{4,7},{9,8},{10,9},{11,1... | collective-permute-start | bytes 50696 | tf_op jit(solution)/shard_map/ppermute | solution.py:23
  42.4 1.7 copy-start
  44.1 0.8 copy-start.2
  45.1 7.0 %collective-permute-start.4 = (f32[8,512]{0,1:T(8,128)S(1)}, f32[8,512]{0,1:T(8,128)S(1)}, u32[]{:S(2)}, u32[]{:S(2)}) collective-permute-start(f32[8,512]{0,1:T(8,128)S(1)} %get-tuple-element.20), channel_id=1, source_target_pairs={{0,4},{1,5},{2,6},{3,7},{8,12},{9,13},{10,14},{11,15},{16,20},{17,... | collective-permute-start | bytes 49160 | tf_op jit(solution)/shard_map/ppermute | solution.py:20
  47.0 9.2 %collective-permute-start.5 = (f32[8,512]{0,1:T(8,128)S(1)}, f32[8,512]{0,1:T(8,128)S(1)}, u32[]{:S(2)}, u32[]{:S(2)}) collective-permute-start(f32[8,512]{0,1:T(8,128)S(1)} %get-tuple-element.21), channel_id=1, source_target_pairs={{4,0},{5,1},{6,2},{7,3},{12,8},{13,9},{14,10},{15,11},{20,16},{21,... | collective-permute-start | bytes 49160 | tf_op jit(solution)/shard_map/ppermute | solution.py:23
  56.2 3.9 %copy-start.7 = (f32[8,512]{0,1:T(8,128)}, f32[8,512]{0,1:T(8,128)S(1)}, u32[]{:S(2)}) copy-start(f32[8,512]{0,1:T(8,128)S(1)} %collective-permute-done.5) | copy-start | bytes 49156
  56.3 6.1 %collective-permute-start.6 = (f32[528,8]{0,1:T(8,128)S(1)}, f32[528,8]{0,1:T(8,128)S(1)}, u32[]{:S(2)}, u32[]{:S(2)}) collective-permute-start(f32[528,8]{0,1:T(8,128)S(1)} %get-tuple-element.10), channel_id=1, source_target_pairs={{0,1},{1,2},{2,3},{3,0},{4,5},{5,6},{6,7},{7,4},{8,9},{9,10},{10,1... | collective-permute-start | bytes 50696 | tf_op jit(solution)/shard_map/ppermute | solution.py:20
  58.1 4.2 %collective-permute-start.7 = (f32[528,8]{0,1:T(8,128)S(1)}, f32[528,8]{0,1:T(8,128)S(1)}, u32[]{:S(2)}, u32[]{:S(2)}) collective-permute-start(f32[528,8]{0,1:T(8,128)S(1)} %get-tuple-element.11), channel_id=1, source_target_pairs={{1,0},{2,1},{3,2},{0,3},{5,4},{6,5},{7,6},{4,7},{9,8},{10,9},{11,1... | collective-permute-start | bytes 50696 | tf_op jit(solution)/shard_map/ppermute | solution.py:23
  126.6 8.9 %collective-permute-start.8 = (f32[8,512]{0,1:T(8,128)S(1)}, f32[8,512]{0,1:T(8,128)S(1)}, u32[]{:S(2)}, u32[]{:S(2)}) collective-permute-start(f32[8,512]{0,1:T(8,128)S(1)} %get-tuple-element.16), channel_id=1, source_target_pairs={{0,4},{1,5},{2,6},{3,7},{8,12},{9,13},{10,14},{11,15},{16,20},{17,... | collective-permute-start | bytes 49160 | tf_op jit(solution)/shard_map/ppermute | solution.py:20
  130.0 9.6 %collective-permute-start.9 = (f32[8,512]{0,1:T(8,128)S(1)}, f32[8,512]{0,1:T(8,128)S(1)}, u32[]{:S(2)}, u32[]{:S(2)}) collective-permute-start(f32[8,512]{0,1:T(8,128)S(1)} %get-tuple-element.17), channel_id=1, source_target_pairs={{4,0},{5,1},{6,2},{7,3},{12,8},{13,9},{14,10},{15,11},{20,16},{21,... | collective-permute-start | bytes 49160 | tf_op jit(solution)/shard_map/ppermute | solution.py:23
  139.6 5.6 %collective-permute-start.10 = (f32[528,8]{0,1:T(8,128)S(1)}, f32[528,8]{0,1:T(8,128)S(1)}, u32[]{:S(2)}, u32[]{:S(2)}) collective-permute-start(f32[528,8]{0,1:T(8,128)S(1)} %get-tuple-element.8), channel_id=1, source_target_pairs={{0,1},{1,2},{2,3},{3,0},{4,5},{5,6},{6,7},{7,4},{8,9},{9,10},{10,1... | collective-permute-start | bytes 50696 | tf_op jit(solution)/shard_map/ppermute | solution.py:20
  141.1 4.1 %collective-permute-start.11 = (f32[528,8]{0,1:T(8,128)S(1)}, f32[528,8]{0,1:T(8,128)S(1)}, u32[]{:S(2)}, u32[]{:S(2)}) collective-permute-start(f32[528,8]{0,1:T(8,128)S(1)} %get-tuple-element.9), channel_id=1, source_target_pairs={{1,0},{2,1},{3,2},{0,3},{5,4},{6,5},{7,6},{4,7},{9,8},{10,9},{11,1... | collective-permute-start | bytes 50696 | tf_op jit(solution)/shard_map/ppermute | solution.py:23
  151.0 1.8 copy-start.1
  151.0 1.8 copy-start.3
  153.7 5.5 %collective-permute-start.12 = (f32[8,512]{0,1:T(8,128)S(1)}, f32[8,512]{0,1:T(8,128)S(1)}, u32[]{:S(2)}, u32[]{:S(2)}) collective-permute-start(f32[8,512]{0,1:T(8,128)S(1)} %get-tuple-element.14), channel_id=1, source_target_pairs={{0,4},{1,5},{2,6},{3,7},{8,12},{9,13},{10,14},{11,15},{16,20},{17,... | collective-permute-start | bytes 49160 | tf_op jit(solution)/shard_map/ppermute | solution.py:20
  155.4 8.3 %collective-permute-start.13 = (f32[8,512]{0,1:T(8,128)S(1)}, f32[8,512]{0,1:T(8,128)S(1)}, u32[]{:S(2)}, u32[]{:S(2)}) collective-permute-start(f32[8,512]{0,1:T(8,128)S(1)} %get-tuple-element.15), channel_id=1, source_target_pairs={{4,0},{5,1},{6,2},{7,3},{12,8},{13,9},{14,10},{15,11},{20,16},{21,... | collective-permute-start | bytes 49160 | tf_op jit(solution)/shard_map/ppermute | solution.py:23
  163.7 4.0 %copy-start.5 = (f32[8,512]{0,1:T(8,128)}, f32[8,512]{0,1:T(8,128)S(1)}, u32[]{:S(2)}) copy-start(f32[8,512]{0,1:T(8,128)S(1)} %collective-permute-done.13) | copy-start | bytes 49156
  163.7 6.0 %collective-permute-start.14 = (f32[528,8]{0,1:T(8,128)S(1)}, f32[528,8]{0,1:T(8,128)S(1)}, u32[]{:S(2)}, u32[]{:S(2)}) collective-permute-start(f32[528,8]{0,1:T(8,128)S(1)} %get-tuple-element.6), channel_id=1, source_target_pairs={{0,1},{1,2},{2,3},{3,0},{4,5},{5,6},{6,7},{7,4},{8,9},{9,10},{10,1... | collective-permute-start | bytes 50696 | tf_op jit(solution)/shard_map/ppermute | solution.py:20
  164.9 4.8 %collective-permute-start.15 = (f32[528,8]{0,1:T(8,128)S(1)}, f32[528,8]{0,1:T(8,128)S(1)}, u32[]{:S(2)}, u32[]{:S(2)}) collective-permute-start(f32[528,8]{0,1:T(8,128)S(1)} %get-tuple-element.7), channel_id=1, source_target_pairs={{1,0},{2,1},{3,2},{0,3},{5,4},{6,5},{7,6},{4,7},{9,8},{10,9},{11,1... | collective-permute-start | bytes 50696 | tf_op jit(solution)/shard_map/ppermute | solution.py:23
  168.4 1.3 copy-start.6
Sparse Core Ops, SparseCore 0:
  72.6 51.6 all-reduce.2
where the time goes:
time: 186 us
  waiting for transfers between devices  90.4 us (49%)
  starting transfers between devices  32.4 us (17%)
  matrix products  29.1 us (16%)
  between operations  15.1 us (8%)
  other arithmetic  12.7 us (7%)
  local copies, waits for them, and re-layouts  5.92 us (3%)
    psum x1, waiting for transfers between devices, per_device(): lax.psum((weight * logb, upstream * jnp.exp(-PHI * logb)), 'hour')  51.8 us
    ppermute x8, waiting for transfers between devices, with_halo(): lax.ppermute(lax.slice_in_dim(block, 0, width, axis=dim), axis, backward)  19.6 us
    ppermute x8, waiting for transfers between devices, with_halo(): lax.ppermute(lax.slice_in_dim(block, block.shape[dim] - width, None, axis...  18.9 us
    ppermute x8, starting transfers between devices, with_halo(): lax.ppermute(lax.slice_in_dim(block, block.shape[dim] - width, None, axis...  17.9 us
    dot_general x8, matrix products, pass_rows(): jnp.dot(band_matrix(size), padded[start:start + size + 2 * RADIUS], preci...  15.1 us
    ppermute x8, starting transfers between devices, with_halo(): lax.ppermute(lax.slice_in_dim(block, 0, width, axis=dim), axis, backward)  14.5 us
    dot_general x8, matrix products, pass_cols(): jnp.dot(padded[:, start:start + size + 2 * RADIUS], band_matrix(size).T,...  13.9 us
    unnamed x22, local copies, waits for them, and re-layouts  4.68 us
  transfers between devices with their start and end apart: 17, of which 12 were waited for; matrix products, arithmetic and copies ran while one was open for 3% of the time, Pallas kernels for 0%

commit v1 on v0

v1 whole, which is shorter than its diff:
```python
import functools
import math
import jax
import jax.numpy as jnp
from jax import lax
from jax.experimental import pallas as pl
from jax.experimental.pallas import tpu as pltpu
from jax.sharding import PartitionSpec as P

RADIUS = 8
PHI = 0.8
SPREAD = 50.0
STEP = 128
EDGE = 2 * RADIUS
TOTAL = sum(math.exp(-d * d / SPREAD) for d in range(-RADIUS, RADIUS + 1))
MESH = pl.DeviceIdType.MESH
F32, BF16 = jnp.float32, jnp.bfloat16
TALL = STEP + 3 * EDGE


def split(x):
    high = x.astype(BF16)
    return high, (x - high.astype(F32)).astype(BF16)


def band(rows, cols, shift):
    i = lax.broadcasted_iota(jnp.int32, (rows, cols), 0)
    j = lax.broadcasted_iota(jnp.int32, (rows, cols), 1)
    d = (j - i - shift).astype(F32)
    return jnp.where(jnp.abs(d) <= RADIUS, jnp.exp(-d * d / SPREAD) / TOTAL, 0.0)


def dot(a, b):
    return jnp.dot(a, b, preferred_element_type=F32)


def kernel(
    sizes, p_hbm, s_hbm, w_ref, c_hbm, gp_hbm, gs_hbm,
    es, ep, ct, first, lift, ds, own, got, part, other, both, scale,
    st_l, st_r, h_l, h_r, sd_l, sd_r, hd_l, hd_r, o_p, o_s,
    t_hi, t_lo, b_hi, b_lo, local, sends, recvs,
):
    n_hour, n_lat, n_lon, rows, cols = sizes
    chunks = rows // STEP
    tall, wide = rows + 2 * EDGE, cols + STEP
    bits = n_hour.bit_length() - 1
    hour, lat, lon = (lax.axis_index(a) for a in ("hour", "lat", "lon"))
    side = lax.rem(hour, 2)
    up, down = lax.rem(lat + n_lat - 1, n_lat), lax.rem(lat + 1, n_lat)
    left, right = lax.rem(lon + n_lon - 1, n_lon), lax.rem(lon + 1, n_lon)

    def flip(bit):
        m = 1 << bit
        return hour + m - 2 * m * lax.rem(hour // m, 2)

    loads = [
        pltpu.make_async_copy(s_hbm.at[0], es.at[pl.ds(EDGE, rows), pl.ds(0, cols)], local.at[0]),
        pltpu.make_async_copy(p_hbm.at[0], ep.at[pl.ds(EDGE, rows), pl.ds(0, cols)], local.at[1]),
        pltpu.make_async_copy(c_hbm.at[0], ct, local.at[2]),
    ]
    for copy in loads:
        copy.start()

    barrier = pltpu.get_barrier_semaphore()
    lats = [up, down] if n_lat > 2 else [down]
    lons = [left, right] if n_lon > 2 else [right]
    peers = [{"lon": z} for z in lons] + [{"lat": x} for x in lats]
    peers += [{"lat": x, "lon": z} for x in lats for z in lons]
    peers += [{"hour": flip(bit)} for bit in range(bits)]
    for peer in peers:
        pl.semaphore_signal(barrier, inc=1, device_id=peer, device_id_type=MESH)

    hi, lo = split(band(t_hi.shape[0], t_hi.shape[1], -STEP).astype(F32))
    t_hi[...], t_lo[...] = hi, lo
    hi, lo = split(band(b_hi.shape[0], b_hi.shape[1], RADIUS))
    b_hi[...], b_lo[...] = hi, lo

    pl.semaphore_wait(barrier, len(peers))

    sent = []

    def send(src, dst, peer):
        at = len(sent)
        copy = pltpu.make_async_remote_copy(
            src_ref=src, dst_ref=dst, send_sem=sends.at[at], recv_sem=recvs.at[at],
            device_id=peer, device_id_type=MESH,
        )
        copy.start()
        sent.append(copy)
        return copy

    def row_pass(x, n):
        xh, xl = split(x)
        bh, bl = b_hi[0:n, 0 : n + EDGE], b_lo[0:n, 0 : n + EDGE]
        return dot(bh, xh) + (dot(bh, xl) + dot(bl, xh))

    def col_pass(x, width):
        xh, xl = split(x)
        blocks = wide // STEP
        out = []
        for start in range(0, width, 2 * STEP):
            size = min(2 * STEP, width - start)
            picks = [(start // STEP - 1 + i) % blocks for i in range(size // STEP + 2)]
            a = jnp.concatenate([xh[:, i * STEP : (i + 1) * STEP] for i in picks], axis=1)
            b = jnp.concatenate([xl[:, i * STEP : (i + 1) * STEP] for i in picks], axis=1)
            depth = size + 2 * STEP
            th, tl = t_hi[0:depth, 0:size], t_lo[0:depth, 0:size]
            out.append(dot(a, th) + (dot(b, th) + dot(a, tl)))
        return jnp.concatenate(out, axis=1)

    arrive = []
    for src, dst in ((s_hbm, es), (p_hbm, ep)):
        arrive.append(send(src.at[0, pl.ds(0, EDGE)], dst.at[pl.ds(EDGE + rows, EDGE), pl.ds(0, cols)], {"lat": up}))
        arrive.append(send(src.at[0, pl.ds(rows - EDGE, EDGE)], dst.at[pl.ds(0, EDGE), pl.ds(0, cols)], {"lat": down}))
    loads[0].wait()
    own_rows = pl.ds(EDGE, rows)
    st_l[0:EDGE, :] = es[own_rows, 0:STEP].T[0:EDGE]
    st_r[0:EDGE, :] = es[own_rows, cols - STEP : cols].T[STEP - EDGE :]
    loads[1].wait()
    st_l[EDGE : EDGE + RADIUS, :] = ep[own_rows, 0:STEP].T[0:RADIUS]
    st_r[EDGE : EDGE + RADIUS, :] = ep[own_rows, cols - STEP : cols].T[STEP - RADIUS :]
    first_lanes, last_lanes = pl.ds(0, STEP), pl.ds(rows - STEP, STEP)
    for stage, dst, z in ((st_l, h_r, left), (st_r, h_l, right)):
        arrive.append(send(stage, dst.at[:, pl.ds(STEP, rows)], {"lon": z}))
        arrive.append(send(stage.at[:, first_lanes], dst.at[:, pl.ds(STEP + rows, STEP)], {"lat": up, "lon": z}))
        arrive.append(send(stage.at[:, last_lanes], dst.at[:, pl.ds(0, STEP)], {"lat": down, "lon": z}))
    for copy in arrive:
        copy.wait_recv()
    lanes = rows + 2 * STEP
    ones = jnp.ones((STEP - 2 * EDGE, lanes), F32)
    block = jnp.concatenate([h_r[0:EDGE], ones, h_l[0:EDGE]], axis=0).T
    es[:, cols:wide] = block[STEP - EDGE : STEP + rows + EDGE]
    ones = jnp.ones((STEP - 2 * RADIUS, lanes), F32)
    block = jnp.concatenate([h_r[EDGE:], ones, h_l[EDGE:]], axis=0).T
    ep[:, cols:wide] = block[STEP - EDGE : STEP + rows + EDGE]
    top, bottom = slice(0, EDGE), slice(EDGE + rows, tall)
    es[top, :] = jnp.where(lat > 0, es[top, :], 0.0)
    es[bottom, :] = jnp.where(lat < n_lat - 1, es[bottom, :], 0.0)
    loads[2].wait()
    weight = w_ref[0]

    def forward(c):
        at = c * STEP
        span = slice(at + RADIUS, at + RADIUS + STEP + EDGE)
        a = col_pass(row_pass(es[at : at + STEP + 2 * EDGE, :], STEP + EDGE), wide)
        first[span, :] = a
        u = jnp.exp(PHI * jnp.log(ep[span, :] / a))
        if c == 0 or c == chunks - 1:
            e = lax.broadcasted_iota(jnp.int32, u.shape, 0) + (at + RADIUS)
            inside = ((lat > 0) | (e >= EDGE)) & ((lat < n_lat - 1) | (e < EDGE + rows))
            u = jnp.where(inside, u, 0.0)
        lift[span, :] = u
        b = col_pass(row_pass(u, STEP), cols)
        logb = jnp.log(b)
        mine = slice(at, at + STEP)
        own[0, mine, :] = weight * logb
        own[1, mine, :] = ct[mine, :] * jnp.exp(-PHI * logb)
        scale[mine, :] = PHI / b
        r = pl.ds(at, STEP)
        return send(own.at[1 - side, r], got.at[r], {"hour": flip(0)})

    def join(c, bit, copy):
        copy.wait_recv()
        at = c * STEP
        mine = slice(at, at + STEP)
        r = pl.ds(at, STEP)
        if bit == 0:
            value = own[side, mine, :] + got[mine, :]
        else:
            value = part[bit - 1, mine, :] + other[bit - 1, mine, :]
        if bit == bits - 1:
            both[side, mine, :] = value
            return send(both.at[side, r], both.at[side, r], {"hour": flip(0)})
        part[bit, mine, :] = value
        return send(part.at[bit, r], other.at[bit, r], {"hour": flip(bit + 1)})

    def second(c, copy):
        copy.wait_recv()
        at = c * STEP
        mine = slice(at, at + STEP)
        d = jnp.exp(PHI * both[0, mine, :]) * (weight * both[1, mine, :] - own[1, mine, :]) * scale[mine, :]
        ds[at + EDGE : at + EDGE + STEP, 0:cols] = d
        sd_l[:, mine] = d[:, 0:STEP].T[0:EDGE]
        sd_r[:, mine] = d[:, cols - STEP : cols].T[STEP - EDGE :]
        r = pl.ds(at, STEP)
        main, corner = [], []
        if c == 0:
            corner.append(send(ds.at[pl.ds(EDGE, EDGE), pl.ds(0, cols)], ds.at[pl.ds(EDGE + rows, EDGE), pl.ds(0, cols)], {"lat": up}))
        if c == chunks - 1:
            corner.append(send(ds.at[pl.ds(rows, EDGE), pl.ds(0, cols)], ds.at[pl.ds(0, EDGE), pl.ds(0, cols)], {"lat": down}))
        for stage, dst, z in ((sd_l, hd_r, left), (sd_r, hd_l, right)):
            main.append(send(stage.at[:, r], dst.at[:, pl.ds(STEP + at, STEP)], {"lon": z}))
            if c == 0:
                corner.append(send(stage.at[:, r], dst.at[:, pl.ds(STEP + rows, STEP)], {"lat": up, "lon": z}))
            if c == chunks - 1:
                corner.append(send(stage.at[:, r], dst.at[:, pl.ds(0, STEP)], {"lat": down, "lon": z}))
        return main, corner

    def side_block(i):
        zeros = jnp.zeros((STEP - 2 * EDGE, STEP), F32)
        at = slice(i * STEP, (i + 1) * STEP)
        return jnp.concatenate([hd_r[:, at], zeros, hd_l[:, at]], axis=0).T

    def take_main(c, copies):
        for copy in copies:
            copy.wait_recv()
        ds[EDGE + c * STEP : EDGE + (c + 1) * STEP, cols:wide] = side_block(c + 1)

    def take_corners(copies):
        for copy in copies:
            copy.wait_recv()
        ds[top, cols:wide] = side_block(0)[STEP - EDGE :]
        ds[bottom, cols:wide] = side_block(chunks + 1)[0:EDGE]
        ds[top, :] = jnp.where(lat > 0, ds[top, :], 0.0)
        ds[bottom, :] = jnp.where(lat < n_lat - 1, ds[bottom, :], 0.0)

    stores = []

    def backward(at, n):
        span = slice(at + RADIUS, at + n + 3 * RADIUS)
        d = col_pass(row_pass(ds[at : at + n + 2 * EDGE, :], n + EDGE), wide)
        carried = PHI * d * lift[span, :]
        mine = slice(at, at + n)
        o_p[mine, :] = carried[RADIUS : RADIUS + n, 0:cols] / ep[at + EDGE : at + EDGE + n, 0:cols]
        o_s[mine, :] = col_pass(row_pass(-carried / first[span, :], n), cols)
        r = pl.ds(at, n)
        for src, dst in ((o_p, gp_hbm), (o_s, gs_hbm)):
            copy = pltpu.make_async_copy(src.at[r], dst.at[0, r], local.at[3 + len(stores)])
            copy.start()
            stores.append(copy)

    order = [0, chunks - 1] + list(range(1, chunks - 1))
    moving = {}
    waiting = None
    for c in order:
        moving[c] = forward(c)
        if waiting is not None:
            moving[waiting] = join(waiting, 0, moving[waiting])
        waiting = c
    moving[waiting] = join(waiting, 0, moving[waiting])
    for bit in range(1, bits - 1):
        for c in order:
            moving[c] = join(c, bit, moving[c])
    mains, corners = {}, []
    done = 0
    for c in order:
        if bits > 1:
            moving[c] = join(c, bits - 1, moving[c])
        mains[c], corner = second(c, moving[c])
        corners += corner
        if c not in (0, chunks - 1):
            if done == 0:
                take_main(0, mains[0])
                take_main(chunks - 1, mains[chunks - 1])
                take_corners(corners)
                backward((chunks - 1) * STEP + EDGE, STEP - EDGE)
                backward(0, STEP - EDGE)
                done = STEP - EDGE
            take_main(c, mains[c])
            end = (c + 1) * STEP + (EDGE if c == chunks - 2 else -EDGE)
            backward(done, end - done)
            done = end
    for copy in sent:
        copy.wait_send()
    for copy in stores:
        copy.wait()


def per_device(n_hour, n_lat, n_lon, precip, scaling, hour_weight, cotangent):
    rows, cols = precip.shape[1:]
    tall, wide, lanes = rows + 2 * EDGE, cols + STEP, rows + 2 * STEP
    bits = n_hour.bit_length() - 1
    chunks = rows // STEP
    assert n_hour == 1 << bits and bits > 0 and min(n_lat, n_lon) > 1
    assert rows % STEP == 0 and cols % (2 * STEP) == 0 and chunks > 2
    ext, tile = pltpu.VMEM((tall, wide), F32), pltpu.VMEM((rows, cols), F32)
    pair = pltpu.VMEM((2, rows, cols), F32)
    steps = pltpu.VMEM((max(bits - 1, 1), rows, cols), F32)
    copies = 10 + chunks * (bits + 3) + 6
    out = jax.ShapeDtypeStruct(precip.shape, F32)
    hbm = pl.BlockSpec(memory_space=pl.ANY)
    return pl.pallas_call(
        functools.partial(kernel, (n_hour, n_lat, n_lon, rows, cols)),
        out_shape=(out, out),
        in_specs=[hbm, hbm, pl.BlockSpec(memory_space=pltpu.SMEM), hbm],
        out_specs=(hbm, hbm),
        scratch_shapes=[
            ext, ext, tile, ext, ext, ext, pair, tile, steps, steps, pair, tile,
            pltpu.VMEM((EDGE + RADIUS, rows), F32), pltpu.VMEM((EDGE + RADIUS, rows), F32),
            pltpu.VMEM((EDGE + RADIUS, lanes), F32), pltpu.VMEM((EDGE + RADIUS, lanes), F32),
            pltpu.VMEM((EDGE, rows), F32), pltpu.VMEM((EDGE, rows), F32),
            pltpu.VMEM((EDGE, lanes), F32), pltpu.VMEM((EDGE, lanes), F32),
            tile, tile,
            pltpu.VMEM((4 * STEP, 2 * STEP), BF16), pltpu.VMEM((4 * STEP, 2 * STEP), BF16),
            pltpu.VMEM((TALL, TALL + EDGE), BF16), pltpu.VMEM((TALL, TALL + EDGE), BF16),
            pltpu.SemaphoreType.DMA((3 + 2 * (chunks + 1),)),
            pltpu.SemaphoreType.DMA((copies,)), pltpu.SemaphoreType.DMA((copies,)),
        ],
        compiler_params=pltpu.CompilerParams(
            collective_id=0, has_side_effects=True, vmem_limit_bytes=56 * 1024 * 1024
        ),
    )(precip, scaling, hour_weight, cotangent)


def solution(mesh):
    field = P("hour", "lat", "lon")
    sizes = [mesh.shape[a] for a in ("hour", "lat", "lon")]
    return jax.shard_map(
        functools.partial(per_device, *sizes), mesh=mesh,
        in_specs=(field, field, P("hour"), field), out_specs=(field, field), check_vma=False,
    )
```

time: 186 us -> 53.5 us (0.29)
  waiting for transfers between devices: 90.4 us -> 0 us
  Pallas kernels: 0 us -> 48.7 us
  starting transfers between devices: 32.4 us -> 0 us
  matrix products: 29.1 us -> 0 us
  between operations: 15.1 us -> 1.29 us
  other arithmetic: 12.7 us -> 0 us
  local copies, waits for them, and re-layouts: 5.92 us -> 3.32 us
    psum x1 -> x0, waiting for transfers between devices: 51.8 us -> none  [per_device(): lax.psum((weight * logb, upstream * jnp.exp(-PHI * logb)), 'hour')]
    pallas_call x0 -> x1, Pallas kernels: none -> 48.7 us  [per_device(): pl.pallas_call(functools.partial(kernel, (n_hour, n_lat, n_lon, rows, col...]
    ppermute x16 -> x0, waiting for transfers between devices: 38.6 us -> none  [the longest x8 19.6 us: with_halo(): lax.ppermute(lax.slice_in_dim(block, 0, width, axis=dim), axis, backward)]
    ppermute x16 -> x0, starting transfers between devices: 32.4 us -> none  [the longest x8 17.9 us: with_halo(): lax.ppermute(lax.slice_in_dim(block, block.shape[dim] - width, None, axis...]
    dot_general x16 -> x0, matrix products: 29.1 us -> none  [the longest x8 15.1 us: pass_rows(): jnp.dot(band_matrix(size), padded[start:start + size + 2 * RADIUS], preci...]
    concatenate x4 -> x0, other arithmetic: 3.81 us -> none  [with_halo(): block = jnp.concatenate([low, block, high], axis=dim)]
    div x3 -> x0, other arithmetic: 3.66 us -> none  [the longest x1 2.14 us: per_device(): dsecond = (weight * dlogq - terms) / second]
    slice x4 -> x0, other arithmetic: 2.13 us -> none  [with_halo(): lax.slice_in_dim(block, block.shape[dim] - width, None, axis=dim)]
  transfers between devices with their start and end apart: 17 -> 0, of which waited for: 12 -> 0; matrix products, arithmetic and copies ran while one was open for 3% -> 0% of each run, Pallas kernels for 0% -> 0%
where the time goes in v1:
time: 53.5 us; the launch traced here: 53.3 us
  Pallas kernels  48.7 us (91%)
  local copies, waits for them, and re-layouts  3.32 us (6%)
  between operations  1.29 us (2%)
    pallas_call x1, Pallas kernels, per_device(): pl.pallas_call(functools.partial(kernel, (n_hour, n_lat, n_lon, rows, col...  48.7 us
    unnamed x4, local copies, waits for them, and re-layouts  3.32 us

profile of v1, /device:TPU:0, one launch (start us, length us, event | category | flops | bytes accessed | tf_op | source)
XLA Modules:
  0.0 53.3 jit_solution(1708897591577509952)
XLA Ops:
  1.3 48.7 %shard_map.59 = (f32[1,512,512]{2,1,0:T(8,128)}, f32[1,512,512]{2,1,0:T(8,128)}) custom-call(f32[1,512,512]{2,1,0:T(8,128)} %p_hbm.1, f32[1,512,512]{2,1,0:T(8,128)} %s_hbm.1, f32[1]{0:T(128)S(6)} %copy.8.w_ref, f32[1,512,512]{2,1,0:T(8,128)} %c_hbm.1), custom_call_target="tpu_custom_call" | custom-call | tf_op jit(solution)/shard_map/pallas_call | solution.py:282
  50.0 0.0 copy-start
  50.0 2.4 %copy.9 = f32[1,512,512]{2,1,0:T(8,128)} copy(f32[1,512,512]{2,1,0:T(8,128)} %get-tuple-element.4) | data formatting | bytes 2097152
  52.3 0.0 copy-done
  52.3 1.0 %copy.10 = f32[1,512,512]{2,1,0:T(8,128)} copy(f32[1,512,512]{2,1,0:T(8,128)S(1)} %copy-done) | data formatting | bytes 2097152
Async XLA Ops:
  50.0 2.4 %copy-start = (f32[1,512,512]{2,1,0:T(8,128)S(1)}, f32[1,512,512]{2,1,0:T(8,128)}, u32[]{:S(2)}) copy-start(f32[1,512,512]{2,1,0:T(8,128)} %get-tuple-element.5) | copy-start | bytes 3145732

commit v2 on v1

v2 whole, which is shorter than its diff:
```python
import functools
import math
import jax
import jax.numpy as jnp
from jax import lax
from jax.experimental import pallas as pl
from jax.experimental.pallas import tpu as pltpu
from jax.sharding import PartitionSpec as P

RADIUS = 8
PHI = 0.8
SPREAD = 50.0
STEP = 128
EDGE = 2 * RADIUS
TOTAL = sum(math.exp(-d * d / SPREAD) for d in range(-RADIUS, RADIUS + 1))
MESH = pl.DeviceIdType.MESH
F32, BF16 = jnp.float32, jnp.bfloat16


def split(x):
    high = x.astype(BF16)
    return high, (x - high.astype(F32)).astype(BF16)


def band(rows, cols, shift):
    i = lax.broadcasted_iota(jnp.int32, (rows, cols), 0)
    j = lax.broadcasted_iota(jnp.int32, (rows, cols), 1)
    d = (j - i - shift).astype(F32)
    return jnp.where(jnp.abs(d) <= RADIUS, jnp.exp(-d * d / SPREAD) / TOTAL, 0.0)


def stacked_rows(n):
    j = lax.broadcasted_iota(jnp.int32, (n, 3 * (n + EDGE)), 1)
    parts = []
    for at in range(3):
        full = band(n, 3 * (n + EDGE), RADIUS + at * (n + EDGE))
        high = full.astype(BF16).astype(F32)
        parts.append(full - high if at == 2 else high)
    depth = n + EDGE
    return jnp.where(j < depth, parts[0], jnp.where(j < 2 * depth, parts[1], parts[2])).astype(BF16)


def stacked_cols(size):
    own_high, own_low = split(band(size, size, 0))
    i = lax.broadcasted_iota(jnp.int32, (STEP, size), 0)
    j = lax.broadcasted_iota(jnp.int32, (STEP, size), 1)

    def beside(lane):
        d = (jnp.where(lane >= STEP // 2, lane - STEP, lane + size) - j).astype(F32)
        return jnp.where(jnp.abs(d) <= RADIUS, jnp.exp(-d * d / SPREAD) / TOTAL, 0.0)

    first = beside(i).astype(BF16)
    middle = (i >= STEP // 4) & (i < 3 * STEP // 4)
    moved = beside(jnp.where(i < STEP // 2, i + STEP // 2, i - STEP // 2))
    low = moved - moved.astype(BF16).astype(F32)
    second = jnp.where(middle, low, first.astype(F32)).astype(BF16)
    return jnp.concatenate([own_high, own_high, own_low, first, second], axis=0)


def plan(rows):
    sizes = [STEP // 2] + [STEP] * ((rows - 2 * STEP) // STEP) + [STEP // 2, STEP]
    pieces = [(sum(sizes[:i]), n) for i, n in enumerate(sizes)]
    last = len(pieces) - 1
    return pieces, [0, last] + list(range(1, last))


def heights(rows):
    found = set()
    pieces, _ = plan(rows)
    for _, n in pieces:
        found |= {n, n + EDGE}
    for _, n in regions(rows):
        found |= {n, n + EDGE}
    return sorted(found)


def regions(rows):
    pieces, order = plan(rows)
    last = len(pieces) - 1
    found = [(0, pieces[0][1] - EDGE), (pieces[last][0] + EDGE, pieces[last][1] - EDGE)]
    at = found[0][1]
    for c in order[2:]:
        end = sum(pieces[c]) + (EDGE if c == last - 1 else -EDGE)
        found.append((at, end - at))
        at = end
    return found


def kernel(
    sizes, p_hbm, s_hbm, w_ref, c_hbm, o_p, o_s,
    es, ep, ct, first, lift, ds, own, got, part, other, both, scale,
    st_l, st_r, h_l, h_r, sd_l, sd_r, hd_l, hd_r, t_pair, t_last,
    local, sends, recvs, *bands,
):
    n_hour, n_lat, n_lon, rows, cols = sizes
    pieces, order = plan(rows)
    count = len(pieces)
    by_height = dict(zip(heights(rows), bands))
    tall, wide = rows + 2 * EDGE, cols + STEP
    bits = n_hour.bit_length() - 1
    hour, lat, lon = (lax.axis_index(a) for a in ("hour", "lat", "lon"))
    side = lax.rem(hour, 2)
    up, down = lax.rem(lat + n_lat - 1, n_lat), lax.rem(lat + 1, n_lat)
    left, right = lax.rem(lon + n_lon - 1, n_lon), lax.rem(lon + 1, n_lon)

    def flip(bit):
        m = 1 << bit
        return hour + m - 2 * m * lax.rem(hour // m, 2)

    own_rows = pl.ds(EDGE, rows)
    loads = []
    for z, n in ((0, STEP), (cols - STEP, STEP), (STEP, cols - 2 * STEP)):
        for src, dst in ((s_hbm, es), (p_hbm, ep)):
            lanes = pl.ds(z, n)
            loads.append(pltpu.make_async_copy(src.at[0, :, lanes], dst.at[own_rows, lanes], local.at[len(loads)]))
    loads.append(pltpu.make_async_copy(c_hbm.at[0], ct, local.at[len(loads)]))
    for copy in loads:
        copy.start()

    barrier = pltpu.get_barrier_semaphore()
    lats = [up, down] if n_lat > 2 else [down]
    lons = [left, right] if n_lon > 2 else [right]
    peers = [{"lon": z} for z in lons] + [{"lat": x} for x in lats]
    peers += [{"lat": x, "lon": z} for x in lats for z in lons]
    peers += [{"hour": flip(bit)} for bit in range(bits)]
    for peer in peers:
        pl.semaphore_signal(barrier, inc=1, device_id=peer, device_id_type=MESH)

    t_pair[...] = stacked_cols(2 * STEP)
    t_last[...] = stacked_cols(STEP)
    for n, ref in by_height.items():
        ref[...] = stacked_rows(n)
    sd_l[...] = jnp.zeros_like(sd_l)
    sd_r[...] = jnp.zeros_like(sd_r)

    pl.semaphore_wait(barrier, len(peers))

    sent = []

    def send(src, dst, peer):
        at = len(sent)
        copy = pltpu.make_async_remote_copy(
            src_ref=src, dst_ref=dst, send_sem=sends.at[at], recv_sem=recvs.at[at],
            device_id=peer, device_id_type=MESH,
        )
        copy.start()
        sent.append(copy)
        return copy

    def row_pass(x, n):
        high, low = split(x)
        return jnp.dot(
            by_height[n][...], jnp.concatenate([high, low, high], axis=0), preferred_element_type=F32
        )

    def col_pass(x, width):
        high, low = split(x)
        blocks = wide // STEP
        lane = lax.broadcasted_iota(jnp.int32, (x.shape[0], STEP), 1)
        middle = (lane >= STEP // 4) & (lane < 3 * STEP // 4)
        out = []
        for start in range(0, width, 2 * STEP):
            size = min(2 * STEP, width - start)
            before = (start // STEP - 1) % blocks * STEP
            after = (start + size) // STEP % blocks * STEP
            beside = jnp.where(lane >= STEP // 2, x[:, before : before + STEP], x[:, after : after + STEP])
            near = beside.astype(BF16)
            rounded = near.astype(F32)
            mixed = jnp.where(middle, pltpu.roll(rounded, STEP // 2, 1), beside - rounded).astype(BF16)
            h, l = high[:, start : start + size], low[:, start : start + size]
            weights = t_pair if size == 2 * STEP else t_last
            out.append(jnp.dot(
                jnp.concatenate([h, l, h, near, mixed], axis=1), weights[...], preferred_element_type=F32
            ))
        return jnp.concatenate(out, axis=1)

    arrive = []
    for src, dst in ((s_hbm, es), (p_hbm, ep)):
        arrive.append(send(src.at[0, pl.ds(0, EDGE)], dst.at[pl.ds(EDGE + rows, EDGE), pl.ds(0, cols)], {"lat": up}))
        arrive.append(send(src.at[0, pl.ds(rows - EDGE, EDGE)], dst.at[pl.ds(0, EDGE), pl.ds(0, cols)], {"lat": down}))
    loads[0].wait()
    loads[2].wait()
    st_l[0:EDGE, :] = es[own_rows, 0:STEP].T[0:EDGE]
    st_r[0:EDGE, :] = es[own_rows, cols - STEP : cols].T[STEP - EDGE :]
    loads[1].wait()
    loads[3].wait()
    st_l[EDGE : EDGE + RADIUS, :] = ep[own_rows, 0:STEP].T[0:RADIUS]
    st_r[EDGE : EDGE + RADIUS, :] = ep[own_rows, cols - STEP : cols].T[STEP - RADIUS :]
    first_lanes, last_lanes = pl.ds(0, STEP), pl.ds(rows - STEP, STEP)
    for stage, dst, z in ((st_l, h_r, left), (st_r, h_l, right)):
        arrive.append(send(stage, dst.at[:, pl.ds(STEP, rows)], {"lon": z}))
        arrive.append(send(stage.at[:, first_lanes], dst.at[:, pl.ds(STEP + rows, STEP)], {"lat": up, "lon": z}))
        arrive.append(send(stage.at[:, last_lanes], dst.at[:, pl.ds(0, STEP)], {"lat": down, "lon": z}))
    for copy in loads[4:]:
        copy.wait()
    for copy in arrive:
        copy.wait_recv()
    lanes = rows + 2 * STEP
    ones = jnp.ones((STEP - 2 * EDGE, lanes), F32)
    block = jnp.concatenate([h_r[0:EDGE], ones, h_l[0:EDGE]], axis=0).T
    es[:, cols:wide] = block[STEP - EDGE : STEP + rows + EDGE]
    ones = jnp.ones((STEP - 2 * RADIUS, lanes), F32)
    block = jnp.concatenate([h_r[EDGE:], ones, h_l[EDGE:]], axis=0).T
    ep[:, cols:wide] = block[STEP - EDGE : STEP + rows + EDGE]
    top, bottom = slice(0, EDGE), slice(EDGE + rows, tall)
    es[top, :] = jnp.where(lat > 0, es[top, :], 0.0)
    es[bottom, :] = jnp.where(lat < n_lat - 1, es[bottom, :], 0.0)
    weight = w_ref[0]

    def lifted(c):
        at, n = pieces[c]
        span = slice(at + RADIUS, at + RADIUS + n + EDGE)
        a = col_pass(row_pass(es[at : at + n + 2 * EDGE, :], n + EDGE), wide)
        first[span, :] = a
        u = jnp.exp(PHI * jnp.log(ep[span, :] / a))
        if c == 0 or c == count - 1:
            e = lax.broadcasted_iota(jnp.int32, u.shape, 0) + (at + RADIUS)
            inside = ((lat > 0) | (e >= EDGE)) & ((lat < n_lat - 1) | (e < EDGE + rows))
            u = jnp.where(inside, u, 0.0)
        lift[span, :] = u

    def logs(c):
        at, n = pieces[c]
        b = col_pass(row_pass(lift[at + RADIUS : at + RADIUS + n + EDGE, :], n), cols)
        logb = jnp.log(b)
        mine = slice(at, at + n)
        own[0, mine, :] = weight * logb
        own[1, mine, :] = ct[mine, :] * jnp.exp(-PHI * logb)
        scale[mine, :] = PHI / b
        r = pl.ds(at, n)
        return send(own.at[1 - side, r], got.at[r], {"hour": flip(0)})

    def join(c, bit, copy):
        copy.wait_recv()
        at, n = pieces[c]
        mine = slice(at, at + n)
        r = pl.ds(at, n)
        if bit == 0:
            value = own[side, mine, :] + got[mine, :]
        else:
            value = part[bit - 1, mine, :] + other[bit - 1, mine, :]
        if bit == bits - 1:
            both[side, mine, :] = value
            return send(both.at[side, r], both.at[side, r], {"hour": flip(0)})
        part[bit, mine, :] = value
        return send(part.at[bit, r], other.at[bit, r], {"hour": flip(bit + 1)})

    def second(c, copy):
        copy.wait_recv()
        at, n = pieces[c]
        mine = slice(at, at + n)
        d = jnp.exp(PHI * both[0, mine, :]) * (weight * both[1, mine, :] - own[1, mine, :]) * scale[mine, :]
        ds[at + EDGE : at + EDGE + n, 0:cols] = d
        sd_l[c, :, 0:n] = d[:, 0:STEP].T[0:EDGE]
        sd_r[c, :, 0:n] = d[:, cols - STEP : cols].T[STEP - EDGE :]
        main, corner = [], []
        inner = pl.ds(0, cols)
        if c == 0:
            corner.append(send(ds.at[pl.ds(EDGE, EDGE), inner], ds.at[pl.ds(EDGE + rows, EDGE), inner], {"lat": up}))
        if c == count - 1:
            corner.append(send(ds.at[pl.ds(rows, EDGE), inner], ds.at[pl.ds(0, EDGE), inner], {"lat": down}))
        for stage, dst, z in ((sd_l, hd_r, left), (sd_r, hd_l, right)):
            main.append(send(stage.at[c], dst.at[c + 1], {"lon": z}))
            if c == 0:
                corner.append(send(stage.at[c], dst.at[count + 1], {"lat": up, "lon": z}))
            if c == count - 1:
                corner.append(send(stage.at[c], dst.at[0], {"lat": down, "lon": z}))
        return main, corner

    def side_block(i, n):
        zeros = jnp.zeros((STEP - 2 * EDGE, n), F32)
        return jnp.concatenate([hd_r[i, :, 0:n], zeros, hd_l[i, :, 0:n]], axis=0).T

    def take_main(c, copies):
        for copy in copies:
            copy.wait_recv()
        at, n = pieces[c]
        ds[EDGE + at : EDGE + at + n, cols:wide] = side_block(c + 1, n)

    def take_corners(copies):
        for copy in copies:
            copy.wait_recv()
        n = pieces[count - 1][1]
        ds[top, cols:wide] = side_block(0, n)[n - EDGE :]
        ds[bottom, cols:wide] = side_block(count + 1, pieces[0][1])[0:EDGE]
        ds[top, :] = jnp.where(lat > 0, ds[top, :], 0.0)
        ds[bottom, :] = jnp.where(lat < n_lat - 1, ds[bottom, :], 0.0)

    def backward(at, n):
        span = slice(at + RADIUS, at + n + 3 * RADIUS)
        d = col_pass(row_pass(ds[at : at + n + 2 * EDGE, :], n + EDGE), wide)
        carried = PHI * d * lift[span, :]
        mine = slice(at, at + n)
        o_p[0, mine, :] = carried[RADIUS : RADIUS + n, 0:cols] / ep[at + EDGE : at + EDGE + n, 0:cols]
        o_s[0, mine, :] = col_pass(row_pass(-carried / first[span, :], n), cols)

    moving = {}
    joined = 0
    ahead = 2 if bits == 2 else count
    for i, c in enumerate(order):
        lifted(c)
        if 0 < i <= ahead:
            moving[order[i - 1]] = join(order[i - 1], 0, moving[order[i - 1]])
            joined = i
        moving[c] = logs(c)
    if joined < ahead:
        for c in order[joined:]:
            moving[c] = join(c, 0, moving[c])
        joined = count
    for bit in range(1, bits - 1):
        for c in order:
            moving[c] = join(c, bit, moving[c])
    areas = regions(rows)
    mains, corners = {}, []
    for i, c in enumerate(order):
        if bits > 1:
            moving[c] = join(c, bits - 1, moving[c])
        if joined < count:
            moving[order[joined]] = join(order[joined], 0, moving[order[joined]])
            joined += 1
        mains[c], corner = second(c, moving[c])
        corners += corner
        if i == 2:
            take_main(order[0], mains[order[0]])
            take_main(order[1], mains[order[1]])
            take_corners(corners)
            backward(*areas[0])
            backward(*areas[1])
        if i > 2:
            take_main(order[i - 1], mains[order[i - 1]])
            backward(*areas[i - 1])
    take_main(order[-1], mains[order[-1]])
    backward(*areas[-1])
    for copy in sent:
        copy.wait_send()


def write_out(p_ref, s_ref, p_out, s_out, done):
    copies = [
        pltpu.make_async_copy(p_ref, p_out, done.at[0]),
        pltpu.make_async_copy(s_ref, s_out, done.at[1]),
    ]
    for copy in copies:
        copy.start()
    for copy in copies:
        copy.wait()


def per_device(n_hour, n_lat, n_lon, precip, scaling, hour_weight, cotangent):
    rows, cols = precip.shape[1:]
    tall, wide, lanes = rows + 2 * EDGE, cols + STEP, rows + 2 * STEP
    bits = n_hour.bit_length() - 1
    pieces, _ = plan(rows)
    count = len(pieces)
    assert n_hour == 1 << bits and bits > 0 and min(n_lat, n_lon) > 1
    assert rows % STEP == 0 and cols % (2 * STEP) == 0 and count > 3
    ext, tile = pltpu.VMEM((tall, wide), F32), pltpu.VMEM((rows, cols), F32)
    pair = pltpu.VMEM((2, rows, cols), F32)
    steps = pltpu.VMEM((max(bits - 1, 1), rows, cols), F32)
    copies = 10 + count * (bits + 3) + 6
    out = jax.ShapeDtypeStruct(precip.shape, F32)
    hbm = pl.BlockSpec(memory_space=pl.ANY)
    vmem = pl.BlockSpec(memory_space=pltpu.VMEM)
    held = pltpu.VMEM(precip.shape, F32)
    stage, halo = pltpu.VMEM((EDGE + RADIUS, rows), F32), pltpu.VMEM((EDGE + RADIUS, lanes), F32)
    piece_stage, piece_halo = pltpu.VMEM((count, EDGE, STEP), F32), pltpu.VMEM((count + 2, EDGE, STEP), F32)
    spare = 64 * 2**20 - 2 * 4 * rows * cols - 2**19
    grads = pl.pallas_call(
        functools.partial(kernel, (n_hour, n_lat, n_lon, rows, cols)),
        out_shape=(held, held),
        in_specs=[hbm, hbm, pl.BlockSpec(memory_space=pltpu.SMEM), hbm],
        out_specs=(vmem, vmem),
        scratch_shapes=[
            ext, ext, tile, ext, ext, ext, pair, tile, steps, steps, pair, tile,
            stage, stage, halo, halo, piece_stage, piece_stage, piece_halo, piece_halo,
            pltpu.VMEM((8 * STEP, 2 * STEP), BF16), pltpu.VMEM((5 * STEP, STEP), BF16),
            pltpu.SemaphoreType.DMA((7,)),
            pltpu.SemaphoreType.DMA((copies,)), pltpu.SemaphoreType.DMA((copies,)),
        ] + [pltpu.VMEM((n, 3 * (n + EDGE)), BF16) for n in heights(rows)],
        compiler_params=pltpu.CompilerParams(
            collective_id=0, has_side_effects=True, vmem_limit_bytes=spare
        ),
    )(precip, scaling, hour_weight, cotangent)
    return pl.pallas_call(
        write_out,
        out_shape=(out, out),
        in_specs=[vmem, vmem],
        out_specs=(hbm, hbm),
        scratch_shapes=[pltpu.SemaphoreType.DMA((2,))],
    )(*grads)


def solution(mesh):
    field = P("hour", "lat", "lon")
    sizes = [mesh.shape[a] for a in ("hour", "lat", "lon")]
    return jax.shard_map(
        functools.partial(per_device, *sizes), mesh=mesh,
        in_specs=(field, field, P("hour"), field), out_specs=(field, field), check_vma=False,
    )
```

time: 53.5 us -> 51.2 us (0.957)
  local copies, waits for them, and re-layouts: 3.32 us -> 1.98 us
  Pallas kernels: 48.7 us -> 47.7 us
    pallas_call x1, Pallas kernels: 48.7 us -> 44.9 us  [per_device(): pl.pallas_call(functools.partial(kernel, (n_hour, n_lat, n_lon, rows, col...]
    pallas_call x0 -> x1, Pallas kernels: none -> 2.87 us  [per_device(): pl.pallas_call(write_out, out_shape=(out, out), in_specs=[vmem, vmem], ou...]
    unnamed x4, local copies, waits for them, and re-layouts: 3.32 us -> 1.98 us
where the time goes in v2:
time: 51.2 us; the launch traced here: 51 us
  Pallas kernels  47.7 us (93%)
  local copies, waits for them, and re-layouts  1.98 us (4%)
  between operations  1.29 us (3%)
    pallas_call x1, Pallas kernels, per_device(): pl.pallas_call(functools.partial(kernel, (n_hour, n_lat, n_lon, rows, col...  44.9 us
    pallas_call x1, Pallas kernels, per_device(): pl.pallas_call(write_out, out_shape=(out, out), in_specs=[vmem, vmem], ou...  2.87 us
    unnamed x4, local copies, waits for them, and re-layouts  1.98 us

profile of v2, /device:TPU:0, one launch (start us, length us, event | category | flops | bytes accessed | tf_op | source)
XLA Modules:
  0.0 51.0 jit_solution(7779759140275483667)
XLA Ops:
  1.3 44.9 %shard_map.59 = (f32[1,512,512]{2,1,0:T(8,128)S(1)}, f32[1,512,512]{2,1,0:T(8,128)S(1)}) custom-call(f32[1,512,512]{2,1,0:T(8,128)} %p_hbm.1, f32[1,512,512]{2,1,0:T(8,128)} %s_hbm.1, f32[1]{0:T(128)S(6)} %copy.6.w_ref, f32[1,512,512]{2,1,0:T(8,128)} %c_hbm.1), custom_call_target="tpu_custom_call" | custom-call | tf_op jit(solution)/shard_map/pallas_call | solution.py:368
  46.1 0.0 copy-start
  46.1 1.0 %copy-done = f32[1,512,512]{2,1,0:T(8,128)} copy-done((f32[1,512,512]{2,1,0:T(8,128)}, f32[1,512,512]{2,1,0:T(8,128)S(1)}, u32[]{:S(2)}) %copy-start) | copy-done | bytes 1048600
  47.1 0.0 copy-start.1
  47.1 1.0 %copy-done.1 = f32[1,512,512]{2,1,0:T(8,128)} copy-done((f32[1,512,512]{2,1,0:T(8,128)}, f32[1,512,512]{2,1,0:T(8,128)S(1)}, u32[]{:S(2)}) %copy-start.1) | copy-done | bytes 1048600
  48.1 2.9 %shard_map.60 = (f32[1,512,512]{2,1,0:T(8,128)}, f32[1,512,512]{2,1,0:T(8,128)}) custom-call(f32[1,512,512]{2,1,0:T(8,128)} %copy-done, f32[1,512,512]{2,1,0:T(8,128)} %copy-done.1), custom_call_target="tpu_custom_call" | custom-call | tf_op jit(solution)/shard_map/pallas_call | solution.py:384
Async XLA Ops:
  46.1 1.0 %copy-start = (f32[1,512,512]{2,1,0:T(8,128)}, f32[1,512,512]{2,1,0:T(8,128)S(1)}, u32[]{:S(2)}) copy-start(f32[1,512,512]{2,1,0:T(8,128)S(1)} %get-tuple-element.4.p_ref) | copy-start | bytes 3145732
  47.1 1.0 %copy-start.1 = (f32[1,512,512]{2,1,0:T(8,128)}, f32[1,512,512]{2,1,0:T(8,128)S(1)}, u32[]{:S(2)}) copy-start(f32[1,512,512]{2,1,0:T(8,128)S(1)} %get-tuple-element.5.s_ref) | copy-start | bytes 3145732

commit v3 on v2

v3 whole, which is shorter than its diff:
```python
import functools
import math
import jax
import jax.numpy as jnp
from jax import lax
from jax.experimental import pallas as pl
from jax.experimental.pallas import tpu as pltpu
from jax.sharding import PartitionSpec as P

RADIUS = 8
PHI = 0.8
SPREAD = 50.0
STEP = 128
EDGE = 2 * RADIUS
TOTAL = sum(math.exp(-d * d / SPREAD) for d in range(-RADIUS, RADIUS + 1))
MESH = pl.DeviceIdType.MESH
F32, BF16 = jnp.float32, jnp.bfloat16


def split(x):
    high = x.astype(BF16)
    return high, (x - high.astype(F32)).astype(BF16)


def taps(d):
    d = d.astype(F32)
    return jnp.where(jnp.abs(d) <= RADIUS, jnp.exp(-d * d / SPREAD) / TOTAL, 0.0)


def either(k, low):
    high = k.astype(BF16).astype(F32)
    return jnp.where(low, k - high, high).astype(BF16)


def places(rows, cols):
    return [lax.broadcasted_iota(jnp.int32, (rows, cols), at) for at in (0, 1)]


def stacked_rows(n):
    depth = n + EDGE
    i, j = places(n, 3 * depth)
    third = j >= 2 * depth
    at = jnp.where(third, j - 2 * depth, jnp.where(j >= depth, j - depth, j))
    return either(taps(at - i - RADIUS), third)


def stacked_cols(size):
    i, j = places(size, size)
    high, low = split(taps(i - j))
    i, j = places(2 * STEP, size)
    middle = (i >= STEP + STEP // 4) & (i < STEP + 3 * STEP // 4)
    lane = jnp.where(i >= STEP, i - STEP, i)
    lane = jnp.where(middle, jnp.where(lane >= STEP // 2, lane - STEP // 2, lane + STEP // 2), lane)
    near = taps(jnp.where(lane >= STEP // 2, lane - STEP, lane + size) - j)
    return jnp.concatenate([high, high, low, either(near, middle)], axis=0)


def row_pass(weights, x):
    high, low = split(x)
    return jnp.dot(weights[...], jnp.concatenate([high, low, high], axis=0), preferred_element_type=F32)


def col_pass(pair, last, x, width):
    high, low = split(x)
    blocks = x.shape[1] // STEP
    lane = lax.broadcasted_iota(jnp.int32, (x.shape[0], STEP), 1)
    middle = (lane >= STEP // 4) & (lane < 3 * STEP // 4)
    out = []
    for start in range(0, width, 2 * STEP):
        size = min(2 * STEP, width - start)
        before = (start // STEP - 1) % blocks * STEP
        after = (start + size) // STEP % blocks * STEP
        beside = jnp.where(lane >= STEP // 2, x[:, before : before + STEP], x[:, after : after + STEP])
        near = beside.astype(BF16)
        rounded = near.astype(F32)
        mixed = jnp.where(middle, pltpu.roll(rounded, STEP // 2, 1), beside - rounded).astype(BF16)
        h, l = high[:, start : start + size], low[:, start : start + size]
        weights = pair if size == 2 * STEP else last
        out.append(jnp.dot(
            jnp.concatenate([h, l, h, near, mixed], axis=1), weights[...], preferred_element_type=F32
        ))
    return jnp.concatenate(out, axis=1)


def backward(at, n, refs, bands):
    ds, first, lift, ep, pair, last = refs
    cols = ds.shape[1] - STEP
    span = slice(at + RADIUS, at + n + 3 * RADIUS)
    d = col_pass(pair, last, row_pass(bands[n + EDGE], ds[at : at + n + 2 * EDGE, :]), ds.shape[1])
    carried = PHI * d * lift[span, :]
    out = carried[RADIUS : RADIUS + n, 0:cols] / ep[at + EDGE : at + EDGE + n, 0:cols]
    return out, col_pass(pair, last, row_pass(bands[n], -carried / first[span, :]), cols)


def plan(rows):
    sizes = [STEP // 2] + [STEP] * ((rows - 2 * STEP) // STEP) + [STEP // 2, STEP]
    pieces = [(sum(sizes[:i]), n) for i, n in enumerate(sizes)]
    last = len(pieces) - 1
    return pieces, [0, last] + list(range(1, last))


def heights(rows):
    found = set()
    pieces, _ = plan(rows)
    for _, n in pieces:
        found |= {n, n + EDGE}
    for _, n in regions(rows):
        found |= {n, n + EDGE}
    return sorted(found)


def regions(rows):
    pieces, order = plan(rows)
    last = len(pieces) - 1
    found = [(0, pieces[0][1] - EDGE), (pieces[last][0] + EDGE, pieces[last][1] - EDGE)]
    at = found[0][1]
    for c in order[2:]:
        end = sum(pieces[c]) + (EDGE if c == last - 1 else -EDGE)
        found.append((at, end - at))
        at = end
    return found


def kernel(sizes, p_hbm, s_hbm, w_ref, c_hbm, *refs):
    heads = heights(sizes[3])
    o_p, o_s, ds, first, lift, ep, *refs = refs
    weights, refs = refs[: 2 + len(heads)], refs[2 + len(heads) :]
    (es, ct, own, got, part, other, both, scale,
     st_l, st_r, h_l, h_r, sd_l, sd_r, hd_l, hd_r, local, sends, recvs) = refs
    t_pair, t_last, *bands = weights
    n_hour, n_lat, n_lon, rows, cols = sizes
    pieces, order = plan(rows)
    count = len(pieces)
    by_height = dict(zip(heads, bands))
    held = (ds, first, lift, ep, t_pair, t_last)
    tall, wide = rows + 2 * EDGE, cols + STEP
    bits = n_hour.bit_length() - 1
    hour, lat, lon = (lax.axis_index(a) for a in ("hour", "lat", "lon"))
    side = lax.rem(hour, 2)
    up, down = lax.rem(lat + n_lat - 1, n_lat), lax.rem(lat + 1, n_lat)
    left, right = lax.rem(lon + n_lon - 1, n_lon), lax.rem(lon + 1, n_lon)

    def flip(bit):
        m = 1 << bit
        return hour + m - 2 * m * lax.rem(hour // m, 2)

    own_rows = pl.ds(EDGE, rows)
    loads = []
    for z, n in ((0, STEP), (cols - STEP, STEP), (STEP, cols - 2 * STEP)):
        for src, dst in ((s_hbm, es), (p_hbm, ep)):
            lanes = pl.ds(z, n)
            loads.append(pltpu.make_async_copy(src.at[0, :, lanes], dst.at[own_rows, lanes], local.at[len(loads)]))
    loads.append(pltpu.make_async_copy(c_hbm.at[0], ct, local.at[len(loads)]))
    for copy in loads:
        copy.start()

    barrier = pltpu.get_barrier_semaphore()
    lats = [up, down] if n_lat > 2 else [down]
    lons = [left, right] if n_lon > 2 else [right]
    peers = [{"lon": z} for z in lons] + [{"lat": x} for x in lats]
    peers += [{"lat": x, "lon": z} for x in lats for z in lons]
    peers += [{"hour": flip(bit)} for bit in range(bits)]
    for peer in peers:
        pl.semaphore_signal(barrier, inc=1, device_id=peer, device_id_type=MESH)

    sd_l[...] = jnp.zeros_like(sd_l)
    sd_r[...] = jnp.zeros_like(sd_r)
    pl.semaphore_wait(barrier, len(peers))

    sent = []

    def send(src, dst, peer):
        at = len(sent)
        copy = pltpu.make_async_remote_copy(
            src_ref=src, dst_ref=dst, send_sem=sends.at[at], recv_sem=recvs.at[at],
            device_id=peer, device_id_type=MESH,
        )
        copy.start()
        sent.append(copy)
        return copy

    def fill(at, n):
        r, lanes = slice(EDGE + at, EDGE + at + n), slice(at, at + n)
        st_l[0:EDGE, lanes] = es[r, 0:STEP].T[0:EDGE]
        st_r[0:EDGE, lanes] = es[r, cols - STEP : cols].T[STEP - EDGE :]
        st_l[EDGE:, lanes] = ep[r, 0:STEP].T[0:RADIUS]
        st_r[EDGE:, lanes] = ep[r, cols - STEP : cols].T[STEP - RADIUS :]

    early, late = [], []
    for src, dst in ((s_hbm, es), (p_hbm, ep)):
        early.append(send(src.at[0, pl.ds(rows - EDGE, EDGE)], dst.at[pl.ds(0, EDGE), pl.ds(0, cols)], {"lat": down}))
    for copy in loads[:4]:
        copy.wait()
    fill(0, STEP)
    fill(rows - STEP, STEP)
    first_lanes, last_lanes = pl.ds(0, STEP), pl.ds(rows - STEP, STEP)
    sides = ((st_l, h_r, left), (st_r, h_l, right))
    for stage, dst, z in sides:
        early.append(send(stage.at[:, first_lanes], dst.at[:, pl.ds(STEP, STEP)], {"lon": z}))
        early.append(send(stage.at[:, last_lanes], dst.at[:, first_lanes], {"lat": down, "lon": z}))
    fill(STEP, rows - 2 * STEP)
    for stage, dst, z in sides:
        late.append(send(stage.at[:, first_lanes], dst.at[:, pl.ds(STEP + rows, STEP)], {"lat": up, "lon": z}))
        late.append(send(stage.at[:, pl.ds(STEP, rows - STEP)], dst.at[:, pl.ds(2 * STEP, rows - STEP)], {"lon": z}))
    for src, dst in ((s_hbm, es), (p_hbm, ep)):
        late.append(send(src.at[0, pl.ds(0, EDGE)], dst.at[pl.ds(EDGE + rows, EDGE), pl.ds(0, cols)], {"lat": up}))

    top, bottom = slice(0, EDGE), slice(EDGE + rows, tall)

    def beside(at, n, start, skip, size):
        lanes = slice(at, at + n)
        for dst, low, high in ((es, 0, EDGE), (ep, EDGE, EDGE + RADIUS)):
            ones = jnp.ones((STEP - 2 * (high - low), n), F32)
            block = jnp.concatenate([h_r[low:high, lanes], ones, h_l[low:high, lanes]], axis=0).T
            dst[start : start + size, cols:wide] = block[skip : skip + size]

    weight = w_ref[0]
    t_pair[...] = stacked_cols(2 * STEP)
    t_last[...] = stacked_cols(STEP)
    for n, ref in by_height.items():
        ref[...] = stacked_rows(n)
    for copy in loads[4:]:
        copy.wait()
    for copy in early:
        copy.wait_recv()
    beside(0, 2 * STEP, 0, STEP - EDGE, STEP + EDGE)
    es[top, :] = jnp.where(lat > 0, es[top, :], 0.0)

    def rest():
        for copy in late:
            copy.wait_recv()
        beside(2 * STEP, rows, STEP + EDGE, 0, rows - STEP + EDGE)
        es[bottom, :] = jnp.where(lat < n_lat - 1, es[bottom, :], 0.0)

    def lifted(c):
        at, n = pieces[c]
        span = slice(at + RADIUS, at + RADIUS + n + EDGE)
        a = col_pass(t_pair, t_last, row_pass(by_height[n + EDGE], es[at : at + n + 2 * EDGE, :]), wide)
        first[span, :] = a
        u = jnp.exp(PHI * jnp.log(ep[span, :] / a))
        if c == 0 or c == count - 1:
            e = lax.broadcasted_iota(jnp.int32, u.shape, 0) + (at + RADIUS)
            inside = ((lat > 0) | (e >= EDGE)) & ((lat < n_lat - 1) | (e < EDGE + rows))
            u = jnp.where(inside, u, 0.0)
        lift[span, :] = u

    def logs(c):
        at, n = pieces[c]
        b = col_pass(t_pair, t_last, row_pass(by_height[n], lift[at + RADIUS : at + RADIUS + n + EDGE, :]), cols)
        logb = jnp.log(b)
        mine = slice(at, at + n)
        own[0, mine, :] = weight * logb
        own[1, mine, :] = ct[mine, :] * jnp.exp(-PHI * logb)
        scale[mine, :] = PHI / b
        r = pl.ds(at, n)
        return send(own.at[1 - side, r], got.at[r], {"hour": flip(0)})

    def join(c, bit, copy):
        copy.wait_recv()
        at, n = pieces[c]
        mine = slice(at, at + n)
        r = pl.ds(at, n)
        if bit == 0:
            value = own[side, mine, :] + got[mine, :]
        else:
            value = part[bit - 1, mine, :] + other[bit - 1, mine, :]
        if bit == bits - 1:
            both[side, mine, :] = value
            return send(both.at[side, r], both.at[side, r], {"hour": flip(0)})
        part[bit, mine, :] = value
        return send(part.at[bit, r], other.at[bit, r], {"hour": flip(bit + 1)})

    def second(c, copy):
        copy.wait_recv()
        at, n = pieces[c]
        mine = slice(at, at + n)
        d = jnp.exp(PHI * both[0, mine, :]) * (weight * both[1, mine, :] - own[1, mine, :]) * scale[mine, :]
        ds[at + EDGE : at + EDGE + n, 0:cols] = d
        sd_l[c, :, 0:n] = d[:, 0:STEP].T[0:EDGE]
        sd_r[c, :, 0:n] = d[:, cols - STEP : cols].T[STEP - EDGE :]
        main, corner = [], []
        inner = pl.ds(0, cols)
        if c == 0:
            corner.append(send(ds.at[pl.ds(EDGE, EDGE), inner], ds.at[pl.ds(EDGE + rows, EDGE), inner], {"lat": up}))
        if c == count - 1:
            corner.append(send(ds.at[pl.ds(rows, EDGE), inner], ds.at[pl.ds(0, EDGE), inner], {"lat": down}))
        for stage, dst, z in ((sd_l, hd_r, left), (sd_r, hd_l, right)):
            main.append(send(stage.at[c], dst.at[c + 1], {"lon": z}))
            if c == 0:
                corner.append(send(stage.at[c], dst.at[count + 1], {"lat": up, "lon": z}))
            if c == count - 1:
                corner.append(send(stage.at[c], dst.at[0], {"lat": down, "lon": z}))
        return main, corner

    def side_block(i, n):
        zeros = jnp.zeros((STEP - 2 * EDGE, n), F32)
        return jnp.concatenate([hd_r[i, :, 0:n], zeros, hd_l[i, :, 0:n]], axis=0).T

    def take_main(c, copies):
        for copy in copies:
            copy.wait_recv()
        at, n = pieces[c]
        ds[EDGE + at : EDGE + at + n, cols:wide] = side_block(c + 1, n)

    def take_corners(copies):
        for copy in copies:
            copy.wait_recv()
        n = pieces[count - 1][1]
        ds[top, cols:wide] = side_block(0, n)[n - EDGE :]
        ds[bottom, cols:wide] = side_block(count + 1, pieces[0][1])[0:EDGE]
        ds[top, :] = jnp.where(lat > 0, ds[top, :], 0.0)
        ds[bottom, :] = jnp.where(lat < n_lat - 1, ds[bottom, :], 0.0)

    def finish(at, n):
        mine = slice(at, at + n)
        o_p[0, mine, :], o_s[0, mine, :] = backward(at, n, held, by_height)

    moving = {}
    joined = 0
    ahead = 3 if bits == 2 else count
    for i, c in enumerate(order):
        lifted(c)
        if 0 < i <= ahead:
            moving[order[i - 1]] = join(order[i - 1], 0, moving[order[i - 1]])
            joined = i
        moving[c] = logs(c)
        if i == 0:
            rest()
    if joined < ahead:
        for c in order[joined:]:
            moving[c] = join(c, 0, moving[c])
        joined = count
    for bit in range(1, bits - 1):
        for c in order:
            moving[c] = join(c, bit, moving[c])
    areas = regions(rows)
    mains, corners = {}, []
    for i, c in enumerate(order):
        if bits > 1:
            moving[c] = join(c, bits - 1, moving[c])
        if joined < count:
            moving[order[joined]] = join(order[joined], 0, moving[order[joined]])
            joined += 1
        mains[c], corner = second(c, moving[c])
        corners += corner
        if i == 2:
            take_main(order[0], mains[order[0]])
            take_main(order[1], mains[order[1]])
            take_corners(corners)
            finish(*areas[0])
            finish(*areas[1])
        if i > 2:
            take_main(order[i - 1], mains[order[i - 1]])
            finish(*areas[i - 1])
    take_main(order[-1], mains[order[-1]])
    for copy in sent:
        copy.wait_send()


def write_out(area, p_ref, s_ref, ds, first, lift, ep, t_pair, t_last, low, high, p_out, s_out, p_last, s_last, done):
    at, n = area
    rows = p_ref.shape[1]
    copies = []

    def write(src, dst):
        copies.append(pltpu.make_async_copy(src, dst, done.at[len(copies)]))
        copies[-1].start()

    for r in (pl.ds(0, at), pl.ds(at + n, rows - at - n)):
        write(p_ref.at[0, r], p_out.at[0, r])
        write(s_ref.at[0, r], s_out.at[0, r])
    refs = (ds, first, lift, ep, t_pair, t_last)
    p_last[...], s_last[...] = backward(at, n, refs, {n: low, n + EDGE: high})
    write(p_last, p_out.at[0, pl.ds(at, n)])
    write(s_last, s_out.at[0, pl.ds(at, n)])
    for copy in copies:
        copy.wait()


def per_device(n_hour, n_lat, n_lon, precip, scaling, hour_weight, cotangent):
    rows, cols = precip.shape[1:]
    tall, wide, lanes = rows + 2 * EDGE, cols + STEP, rows + 2 * STEP
    bits = n_hour.bit_length() - 1
    pieces, _ = plan(rows)
    count = len(pieces)
    assert n_hour == 1 << bits and bits > 0 and min(n_lat, n_lon) > 1
    assert rows % STEP == 0 and cols % (2 * STEP) == 0 and count > 3
    ext, tile = pltpu.VMEM((tall, wide), F32), pltpu.VMEM((rows, cols), F32)
    pair = pltpu.VMEM((2, rows, cols), F32)
    steps = pltpu.VMEM((max(bits - 1, 1), rows, cols), F32)
    copies = 12 + count * (bits + 3) + 6
    out = jax.ShapeDtypeStruct(precip.shape, F32)
    hbm = pl.BlockSpec(memory_space=pl.ANY)
    vmem = pl.BlockSpec(memory_space=pltpu.VMEM)
    held = pltpu.VMEM(precip.shape, F32)
    stage, halo = pltpu.VMEM((EDGE + RADIUS, rows), F32), pltpu.VMEM((EDGE + RADIUS, lanes), F32)
    piece_stage, piece_halo = pltpu.VMEM((count, EDGE, STEP), F32), pltpu.VMEM((count + 2, EDGE, STEP), F32)
    heads = heights(rows)
    fixed = [(8 * STEP, 2 * STEP), (5 * STEP, STEP)] + [(n, 3 * (n + EDGE)) for n in heads]
    held = [pltpu.VMEM(precip.shape, F32)] * 2 + [ext] * 4 + [pltpu.VMEM(k, BF16) for k in fixed]
    size = 4 * (2 * rows * cols + 4 * tall * wide) + sum(2 * k[0] * (-(-k[1] // STEP) * STEP) for k in fixed)
    spare = (64 * 2**20 - size - 2**19) // 1024 * 1024
    made = pl.pallas_call(
        functools.partial(kernel, (n_hour, n_lat, n_lon, rows, cols)),
        out_shape=tuple(held),
        in_specs=[hbm, hbm, pl.BlockSpec(memory_space=pltpu.SMEM), hbm],
        out_specs=tuple([vmem] * len(held)),
        scratch_shapes=[
            ext, tile, pair, tile, steps, steps, pair, tile,
            stage, stage, halo, halo, piece_stage, piece_stage, piece_halo, piece_halo,
            pltpu.SemaphoreType.DMA((7,)),
            pltpu.SemaphoreType.DMA((copies,)), pltpu.SemaphoreType.DMA((copies,)),
        ],
        compiler_params=pltpu.CompilerParams(
            collective_id=0, has_side_effects=True, vmem_limit_bytes=spare
        ),
    )(precip, scaling, hour_weight, cotangent)
    at, n = regions(rows)[-1]
    bands = dict(zip(heads, made[8:]))
    return pl.pallas_call(
        functools.partial(write_out, (at, n)),
        out_shape=(out, out),
        in_specs=[vmem] * 10,
        out_specs=(hbm, hbm),
        scratch_shapes=[
            pltpu.VMEM((n, cols), F32), pltpu.VMEM((n, cols), F32), pltpu.SemaphoreType.DMA((6,)),
        ],
        compiler_params=pltpu.CompilerParams(vmem_limit_bytes=8 * 2**20),
    )(*made[:8], bands[n], bands[n + EDGE])


def solution(mesh):
    field = P("hour", "lat", "lon")
    sizes = [mesh.shape[a] for a in ("hour", "lat", "lon")]
    return jax.shard_map(
        functools.partial(per_device, *sizes), mesh=mesh,
        in_specs=(field, field, P("hour"), field), out_specs=(field, field), check_vma=False,
    )
```

time: 51.2 us -> 47.2 us (0.922)
  local copies, waits for them, and re-layouts: 1.98 us -> 0 us
  Pallas kernels: 47.7 us -> 45.8 us
    unnamed x4 -> x0, local copies, waits for them, and re-layouts: 1.98 us -> none
    pallas_call x1, Pallas kernels: 2.87 us -> 1.89 us  [per_device(): pl.pallas_call(functools.partial(write_out, (at, n)), out_shape=(out, out...]
    pallas_call x1, Pallas kernels: 44.9 us -> 43.9 us  [per_device(): pl.pallas_call(functools.partial(kernel, (n_hour, n_lat, n_lon, rows, col...]
where the time goes in v3:
time: 47.2 us; the launch traced here: 47.1 us
  Pallas kernels  45.8 us (97%)
  between operations  1.28 us (3%)
    pallas_call x1, Pallas kernels, per_device(): pl.pallas_call(functools.partial(kernel, (n_hour, n_lat, n_lon, rows, col...  43.9 us
    pallas_call x1, Pallas kernels, per_device(): pl.pallas_call(functools.partial(write_out, (at, n)), out_shape=(out, out...  1.89 us

profile of v3, /device:TPU:0, one launch (start us, length us, event | category | flops | bytes accessed | tf_op | source)
XLA Modules:
  0.0 47.1 jit_solution(8041547654891694368)
XLA Ops:
  1.3 43.9 %shard_map.59 = (f32[1,512,512]{2,1,0:T(8,128)S(1)}, f32[1,512,512]{2,1,0:T(8,128)S(1)}, f32[544,640]{1,0:T(8,128)S(1)}, f32[544,640]{1,0:T(8,128)S(1)}, f32[544...) custom-call(f32[1,512,512]{2,1,0:T(8,128)} %p_hbm.1, ...), custom_call_target="tpu_custom_call" | custom-call | tf_op jit(solution)/shard_map/pallas_call | solution.py:403
  45.2 1.9 %shard_map.60 = (f32[1,512,512]{2,1,0:T(8,128)}, f32[1,512,512]{2,1,0:T(8,128)}) custom-call(f32[1,512,512]{2,1,0:T(8,128)S(1)} %get-tuple-element.12.p_ref, f32[1,512,512]{2,1,0:T(8,128)S(1)} %get-tuple-element.13.s_ref, f32[544,640]{1,0:T(8,128)S(1)} %get-tuple-element.14.ds, f32[544,640]{1,0:T(8,128)S(1)} %get-tuple-element.15.first, ...), custom_call_target="tpu_custom_call" | custom-call | tf_op jit(solution)/shard_map/pallas_call | solution.py:420

commit v4 on v3

--- a/solution.py
+++ b/solution.py
@@ -11,6 +11,7 @@
 PHI = 0.8
 SPREAD = 50.0
 STEP = 128
+PART = STEP // 2
 EDGE = 2 * RADIUS
 TOTAL = sum(math.exp(-d * d / SPREAD) for d in range(-RADIUS, RADIUS + 1))
 MESH = pl.DeviceIdType.MESH
@@ -99,12 +100,30 @@
     return pieces, [0, last] + list(range(1, last))
 
 
+def split_up(rows):
+    pieces, order = plan(rows)
+    found = []
+    for c in order:
+        at, n = pieces[c]
+        own = list(range(at // PART, (at + n) // PART))
+        found += own[::-1] if c == len(pieces) - 1 else own
+    return found
+
+
+def made_by(rows):
+    pieces, order = plan(rows)
+    found, at = [], -1
+    for c in order:
+        at += pieces[c][1] // PART
+        found.append(at)
+    return found
+
+
 def heights(rows):
     found = set()
-    pieces, _ = plan(rows)
-    for _, n in pieces:
-        found |= {n, n + EDGE}
-    for _, n in regions(rows):
+    spans = plan(rows)[0] + regions(rows)
+    spans.append((0, spans[-2][1] // 2))
+    for _, n in spans:
         found |= {n, n + EDGE}
     return sorted(found)
 
@@ -130,7 +149,8 @@
     t_pair, t_last, *bands = weights
     n_hour, n_lat, n_lon, rows, cols = sizes
     pieces, order = plan(rows)
-    count = len(pieces)
+    parts = split_up(rows)
+    count = len(parts)
     by_height = dict(zip(heads, bands))
     held = (ds, first, lift, ep, t_pair, t_last)
     tall, wide = rows + 2 * EDGE, cols + STEP
@@ -238,7 +258,7 @@
         a = col_pass(t_pair, t_last, row_pass(by_height[n + EDGE], es[at : at + n + 2 * EDGE, :]), wide)
         first[span, :] = a
         u = jnp.exp(PHI * jnp.log(ep[span, :] / a))
-        if c == 0 or c == count - 1:
+        if c == 0 or c == len(pieces) - 1:
             e = lax.broadcasted_iota(jnp.int32, u.shape, 0) + (at + RADIUS)
             inside = ((lat > 0) | (e >= EDGE)) & ((lat < n_lat - 1) | (e < EDGE + rows))
             u = jnp.where(inside, u, 0.0)
@@ -252,62 +272,65 @@
         own[0, mine, :] = weight * logb
         own[1, mine, :] = ct[mine, :] * jnp.exp(-PHI * logb)
         scale[mine, :] = PHI / b
-        r = pl.ds(at, n)
-        return send(own.at[1 - side, r], got.at[r], {"hour": flip(0)})
-
-    def join(c, bit, copy):
-        copy.wait_recv()
-        at, n = pieces[c]
-        mine = slice(at, at + n)
-        r = pl.ds(at, n)
+        for i, q in enumerate(parts):
+            if at <= q * PART < at + n:
+                r = pl.ds(q * PART, PART)
+                moving[i] = send(own.at[1 - side, r], got.at[r], {"hour": flip(0)})
+
+    def join(i, bit):
+        moving[i].wait_recv()
+        at = parts[i] * PART
+        mine = slice(at, at + PART)
+        r = pl.ds(at, PART)
         if bit == 0:
             value = own[side, mine, :] + got[mine, :]
         else:
             value = part[bit - 1, mine, :] + other[bit - 1, mine, :]
         if bit == bits - 1:
             both[side, mine, :] = value
-            return send(both.at[side, r], both.at[side, r], {"hour": flip(0)})
+            moving[i] = send(both.at[side, r], both.at[side, r], {"hour": flip(0)})
+            return
         part[bit, mine, :] = value
-        return send(part.at[bit, r], other.at[bit, r], {"hour": flip(bit + 1)})
-
-    def second(c, copy):
-        copy.wait_recv()
-        at, n = pieces[c]
+        moving[i] = send(part.at[bit, r], other.at[bit, r], {"hour": flip(bit + 1)})
+
+    def second(i):
+        moving[i].wait_recv()
+        c = parts[i]
+        at, n = c * PART, PART
         mine = slice(at, at + n)
         d = jnp.exp(PHI * both[0, mine, :]) * (weight * both[1, mine, :] - own[1, mine, :]) * scale[mine, :]
         ds[at + EDGE : at + EDGE + n, 0:cols] = d
         sd_l[c, :, 0:n] = d[:, 0:STEP].T[0:EDGE]
         sd_r[c, :, 0:n] = d[:, cols - STEP : cols].T[STEP - EDGE :]
-        main, corner = [], []
         inner = pl.ds(0, cols)
         if c == 0:
-            corner.append(send(ds.at[pl.ds(EDGE, EDGE), inner], ds.at[pl.ds(EDGE + rows, EDGE), inner], {"lat": up}))
+            corners.append(send(ds.at[pl.ds(EDGE, EDGE), inner], ds.at[pl.ds(EDGE + rows, EDGE), inner], {"lat": up}))
         if c == count - 1:
-            corner.append(send(ds.at[pl.ds(rows, EDGE), inner], ds.at[pl.ds(0, EDGE), inner], {"lat": down}))
+            corners.append(send(ds.at[pl.ds(rows, EDGE), inner], ds.at[pl.ds(0, EDGE), inner], {"lat": down}))
         for stage, dst, z in ((sd_l, hd_r, left), (sd_r, hd_l, right)):
-            main.append(send(stage.at[c], dst.at[c + 1], {"lon": z}))
+            mains.append((i, send(stage.at[c], dst.at[c + 1], {"lon": z})))
             if c == 0:
-                corner.append(send(stage.at[c], dst.at[count + 1], {"lat": up, "lon": z}))
+                corners.append(send(stage.at[c], dst.at[count + 1], {"lat": up, "lon": z}))
             if c == count - 1:
-                corner.append(send(stage.at[c], dst.at[0], {"lat": down, "lon": z}))
-        return main, corner
-
-    def side_block(i, n):
-        zeros = jnp.zeros((STEP - 2 * EDGE, n), F32)
-        return jnp.concatenate([hd_r[i, :, 0:n], zeros, hd_l[i, :, 0:n]], axis=0).T
-
-    def take_main(c, copies):
-        for copy in copies:
+                corners.append(send(stage.at[c], dst.at[0], {"lat": down, "lon": z}))
+
+    def side_block(i):
+        zeros = jnp.zeros((STEP - 2 * EDGE, PART), F32)
+        return jnp.concatenate([hd_r[i, :, 0:PART], zeros, hd_l[i, :, 0:PART]], axis=0).T
+
+    def take(most):
+        while mains and mains[0][0] <= most:
+            i, copy = mains.pop(0)
             copy.wait_recv()
-        at, n = pieces[c]
-        ds[EDGE + at : EDGE + at + n, cols:wide] = side_block(c + 1, n)
-
-    def take_corners(copies):
-        for copy in copies:
+            if not mains or mains[0][0] != i:
+                at = EDGE + parts[i] * PART
+                ds[at : at + PART, cols:wide] = side_block(parts[i] + 1)
+
+    def take_corners():
+        for copy in corners:
             copy.wait_recv()
-        n = pieces[count - 1][1]
-        ds[top, cols:wide] = side_block(0, n)[n - EDGE :]
-        ds[bottom, cols:wide] = side_block(count + 1, pieces[0][1])[0:EDGE]
+        ds[top, cols:wide] = side_block(0)[PART - EDGE :]
+        ds[bottom, cols:wide] = side_block(count + 1)[0:EDGE]
         ds[top, :] = jnp.where(lat > 0, ds[top, :], 0.0)
         ds[bottom, :] = jnp.where(lat < n_lat - 1, ds[bottom, :], 0.0)
 
@@ -315,44 +338,54 @@
         mine = slice(at, at + n)
         o_p[0, mine, :], o_s[0, mine, :] = backward(at, n, held, by_height)
 
-    moving = {}
-    joined = 0
-    ahead = 3 if bits == 2 else count
-    for i, c in enumerate(order):
-        lifted(c)
-        if 0 < i <= ahead:
-            moving[order[i - 1]] = join(order[i - 1], 0, moving[order[i - 1]])
-            joined = i
-        moving[c] = logs(c)
-        if i == 0:
-            rest()
-    if joined < ahead:
-        for c in order[joined:]:
-            moving[c] = join(c, 0, moving[c])
-        joined = count
-    for bit in range(1, bits - 1):
-        for c in order:
-            moving[c] = join(c, bit, moving[c])
+    moving, mains, corners = {}, [], []
+    lifted(order[0])
+    logs(order[0])
+    rest()
+    started = 0
+    for f in range(1, 3):
+        lifted(order[f])
+        if bits == 2:
+            join(started, 0)
+            started += 1
+        logs(order[f])
+    ready = 3
+    if bits != 2:
+        for c in order[ready:]:
+            lifted(c)
+            logs(c)
+        for bit in range(bits - 1):
+            for i in range(count):
+                join(i, bit)
+        ready, started = len(order), count
     areas = regions(rows)
-    mains, corners = {}, []
-    for i, c in enumerate(order):
-        if bits > 1:
-            moving[c] = join(c, bits - 1, moving[c])
-        if joined < count:
-            moving[order[joined]] = join(order[joined], 0, moving[order[joined]])
-            joined += 1
-        mains[c], corner = second(c, moving[c])
-        corners += corner
-        if i == 2:
-            take_main(order[0], mains[order[0]])
-            take_main(order[1], mains[order[1]])
-            take_corners(corners)
-            finish(*areas[0])
-            finish(*areas[1])
-        if i > 2:
-            take_main(order[i - 1], mains[order[i - 1]])
-            finish(*areas[i - 1])
-    take_main(order[-1], mains[order[-1]])
+    ends = made_by(rows)
+    done = 0
+    for i in range(count):
+        join(i, bits - 1)
+        if started < count:
+            join(started, 0)
+            started += 1
+        while ready < len(order) and ends[ready - 1] < i + 5:
+            lifted(order[ready])
+            logs(order[ready])
+            ready += 1
+        final = i == count - 1
+        if final:
+            at, n = areas[done]
+            take(i - 1)
+            finish(at, n // 2)
+        second(i)
+        if final:
+            finish(at + n // 2, n - n // 2)
+            take(i)
+            continue
+        while done < len(areas) - 2 and ends[max(done, 1)] < i:
+            take(i - 1)
+            if done == 0:
+                take_corners()
+            finish(*areas[done])
+            done += 1
     for copy in sent:
         copy.wait_send()
 
@@ -381,10 +414,9 @@
     rows, cols = precip.shape[1:]
     tall, wide, lanes = rows + 2 * EDGE, cols + STEP, rows + 2 * STEP
     bits = n_hour.bit_length() - 1
-    pieces, _ = plan(rows)
-    count = len(pieces)
+    count = rows // PART
     assert n_hour == 1 << bits and bits > 0 and min(n_lat, n_lon) > 1
-    assert rows % STEP == 0 and cols % (2 * STEP) == 0 and count > 3
+    assert rows % STEP == 0 and cols % (2 * STEP) == 0 and rows >= 4 * STEP
     ext, tile = pltpu.VMEM((tall, wide), F32), pltpu.VMEM((rows, cols), F32)
     pair = pltpu.VMEM((2, rows, cols), F32)
     steps = pltpu.VMEM((max(bits - 1, 1), rows, cols), F32)

time: 47.2 us -> 49.4 us (1.047)
  Pallas kernels: 45.8 us -> 48 us
    pallas_call x1, Pallas kernels: 43.9 us -> 46.1 us  [per_device(): pl.pallas_call(functools.partial(kernel, (n_hour, n_lat, n_lon, rows, col...]
where the time goes in v4:
time: 49.4 us; the launch traced here: 49.3 us
  Pallas kernels  48 us (97%)
  between operations  1.28 us (3%)
    pallas_call x1, Pallas kernels, per_device(): pl.pallas_call(functools.partial(kernel, (n_hour, n_lat, n_lon, rows, col...  46.1 us
    pallas_call x1, Pallas kernels, per_device(): pl.pallas_call(functools.partial(write_out, (at, n)), out_shape=(out, out...  1.89 us

profile of v4, /device:TPU:0, one launch (start us, length us, event | category | flops | bytes accessed | tf_op | source)
XLA Modules:
  0.0 49.3 jit_solution(9449162802860722385)
XLA Ops:
  1.3 46.1 %shard_map.59 = (f32[1,512,512]{2,1,0:T(8,128)S(1)}, f32[1,512,512]{2,1,0:T(8,128)S(1)}, f32[544,640]{1,0:T(8,128)S(1)}, f32[544,640]{1,0:T(8,128)S(1)}, f32[544...) custom-call(f32[1,512,512]{2,1,0:T(8,128)} %p_hbm.1, ...), custom_call_target="tpu_custom_call" | custom-call | tf_op jit(solution)/shard_map/pallas_call | solution.py:435
  47.4 1.9 %shard_map.60 = (f32[1,512,512]{2,1,0:T(8,128)}, f32[1,512,512]{2,1,0:T(8,128)}) custom-call(f32[1,512,512]{2,1,0:T(8,128)S(1)} %get-tuple-element.12.p_ref, f32[1,512,512]{2,1,0:T(8,128)S(1)} %get-tuple-element.13.s_ref, f32[544,640]{1,0:T(8,128)S(1)} %get-tuple-element.14.ds, f32[544,640]{1,0:T(8,128)S(1)} %get-tuple-element.15.first, ...), custom_call_target="tpu_custom_call" | custom-call | tf_op jit(solution)/shard_map/pallas_call | solution.py:452

commit v5 on v4

--- a/solution.py
+++ b/solution.py
@@ -350,7 +350,10 @@
             started += 1
         logs(order[f])
     ready = 3
-    if bits != 2:
+    if bits == 2:
+        join(started, 0)
+        started += 1
+    else:
         for c in order[ready:]:
             lifted(c)
             logs(c)
@@ -366,26 +369,30 @@
         if started < count:
             join(started, 0)
             started += 1
+        if 0 < i < count - 1:
+            second(i - 1)
         while ready < len(order) and ends[ready - 1] < i + 5:
             lifted(order[ready])
             logs(order[ready])
             ready += 1
-        final = i == count - 1
-        if final:
+        if i == count - 1:
             at, n = areas[done]
             take(i - 1)
             finish(at, n // 2)
-        second(i)
-        if final:
+            second(i)
             finish(at + n // 2, n - n // 2)
             take(i)
-            continue
-        while done < len(areas) - 2 and ends[max(done, 1)] < i:
-            take(i - 1)
+            break
+        while done < len(areas) - 2 and ends[max(done, 1)] < i - 1:
+            take(i - 2)
             if done == 0:
                 take_corners()
             finish(*areas[done])
             done += 1
+            if i < count - 2:
+                break
+        if i == count - 2:
+            second(i)
     for copy in sent:
         copy.wait_send()
 

time: 49.4 us -> 50.3 us (1.018)
  Pallas kernels: 48 us -> 48.8 us
    pallas_call x1, Pallas kernels: 46.1 us -> 46.9 us  [per_device(): pl.pallas_call(functools.partial(kernel, (n_hour, n_lat, n_lon, rows, col...]
where the time goes in v5:
time: 50.3 us; the launch traced here: 50.1 us
  Pallas kernels  48.8 us (97%)
  between operations  1.28 us (3%)
    pallas_call x1, Pallas kernels, per_device(): pl.pallas_call(functools.partial(kernel, (n_hour, n_lat, n_lon, rows, col...  46.9 us
    pallas_call x1, Pallas kernels, per_device(): pl.pallas_call(functools.partial(write_out, (at, n)), out_shape=(out, out...  1.9 us

profile of v5, /device:TPU:0, one launch (start us, length us, event | category | flops | bytes accessed | tf_op | source)
XLA Modules:
  0.0 50.1 jit_solution(2584062323250321072)
XLA Ops:
  1.3 46.9 %shard_map.59 = (f32[1,512,512]{2,1,0:T(8,128)S(1)}, f32[1,512,512]{2,1,0:T(8,128)S(1)}, f32[544,640]{1,0:T(8,128)S(1)}, f32[544,640]{1,0:T(8,128)S(1)}, f32[544...) custom-call(f32[1,512,512]{2,1,0:T(8,128)} %p_hbm.1, ...), custom_call_target="tpu_custom_call" | custom-call | tf_op jit(solution)/shard_map/pallas_call | solution.py:442
  48.2 1.9 %shard_map.60 = (f32[1,512,512]{2,1,0:T(8,128)}, f32[1,512,512]{2,1,0:T(8,128)}) custom-call(f32[1,512,512]{2,1,0:T(8,128)S(1)} %get-tuple-element.12.p_ref, f32[1,512,512]{2,1,0:T(8,128)S(1)} %get-tuple-element.13.s_ref, f32[544,640]{1,0:T(8,128)S(1)} %get-tuple-element.14.ds, f32[544,640]{1,0:T(8,128)S(1)} %get-tuple-element.15.first, ...), custom_call_target="tpu_custom_call" | custom-call | tf_op jit(solution)/shard_map/pallas_call | solution.py:459

commit v6 on v3

--- a/solution.py
+++ b/solution.py
@@ -104,7 +104,9 @@
     pieces, _ = plan(rows)
     for _, n in pieces:
         found |= {n, n + EDGE}
-    for _, n in regions(rows):
+    areas = regions(rows)
+    areas.append((0, areas[-2][1] // 2))
+    for _, n in areas:
         found |= {n, n + EDGE}
     return sorted(found)
 
@@ -341,17 +343,24 @@
         if joined < count:
             moving[order[joined]] = join(order[joined], 0, moving[order[joined]])
             joined += 1
+        final = i == count - 1
+        if final:
+            at, n = areas[i - 1]
+            take_main(order[i - 1], mains[order[i - 1]])
+            finish(at, n // 2)
         mains[c], corner = second(c, moving[c])
         corners += corner
-        if i == 2:
+        if final:
+            finish(at + n // 2, n - n // 2)
+        if i == 1:
             take_main(order[0], mains[order[0]])
             take_main(order[1], mains[order[1]])
             take_corners(corners)
             finish(*areas[0])
             finish(*areas[1])
-        if i > 2:
-            take_main(order[i - 1], mains[order[i - 1]])
-            finish(*areas[i - 1])
+        if 1 < i < count - 2:
+            take_main(c, mains[c])
+            finish(*areas[i])
     take_main(order[-1], mains[order[-1]])
     for copy in sent:
         copy.wait_send()

time: 47.2 us -> 50.9 us (1.078)
  Pallas kernels: 45.8 us -> 49.4 us
    pallas_call x1, Pallas kernels: 43.9 us -> 47.5 us  [per_device(): pl.pallas_call(functools.partial(kernel, (n_hour, n_lat, n_lon, rows, col...]
where the time goes in v6:
time: 50.9 us; the launch traced here: 50.7 us
  Pallas kernels  49.4 us (97%)
  between operations  1.28 us (3%)
    pallas_call x1, Pallas kernels, per_device(): pl.pallas_call(functools.partial(kernel, (n_hour, n_lat, n_lon, rows, col...  47.5 us
    pallas_call x1, Pallas kernels, per_device(): pl.pallas_call(functools.partial(write_out, (at, n)), out_shape=(out, out...  1.89 us

profile of v6, /device:TPU:0, one launch (start us, length us, event | category | flops | bytes accessed | tf_op | source)
XLA Modules:
  0.0 50.7 jit_solution(2479030358793114485)
XLA Ops:
  1.3 47.5 %shard_map.59 = (f32[1,512,512]{2,1,0:T(8,128)S(1)}, f32[1,512,512]{2,1,0:T(8,128)S(1)}, f32[544,640]{1,0:T(8,128)S(1)}, f32[544,640]{1,0:T(8,128)S(1)}, f32[544...) custom-call(f32[1,512,512]{2,1,0:T(8,128)} %p_hbm.1, ...), custom_call_target="tpu_custom_call" | custom-call | tf_op jit(solution)/shard_map/pallas_call | solution.py:412
  48.8 1.9 %shard_map.60 = (f32[1,512,512]{2,1,0:T(8,128)}, f32[1,512,512]{2,1,0:T(8,128)}) custom-call(f32[1,512,512]{2,1,0:T(8,128)S(1)} %get-tuple-element.12.p_ref, f32[1,512,512]{2,1,0:T(8,128)S(1)} %get-tuple-element.13.s_ref, f32[544,640]{1,0:T(8,128)S(1)} %get-tuple-element.14.ds, f32[544,640]{1,0:T(8,128)S(1)} %get-tuple-element.15.first, ...), custom_call_target="tpu_custom_call" | custom-call | tf_op jit(solution)/shard_map/pallas_call | solution.py:429

commit v7 on v3

--- a/solution.py
+++ b/solution.py
@@ -341,17 +341,20 @@
         if joined < count:
             moving[order[joined]] = join(order[joined], 0, moving[order[joined]])
             joined += 1
-        mains[c], corner = second(c, moving[c])
-        corners += corner
-        if i == 2:
+        for k in range(max(i - 1, 0), i + 1 if i == count - 1 else i):
+            mains[order[k]], corner = second(order[k], moving[order[k]])
+            corners += corner
+        if i == count - 2:
             take_main(order[0], mains[order[0]])
             take_main(order[1], mains[order[1]])
             take_corners(corners)
             finish(*areas[0])
             finish(*areas[1])
-        if i > 2:
-            take_main(order[i - 1], mains[order[i - 1]])
-            finish(*areas[i - 1])
+            for k in range(2, i):
+                take_main(order[k], mains[order[k]])
+                finish(*areas[k])
+    take_main(order[-2], mains[order[-2]])
+    finish(*areas[-2])
     take_main(order[-1], mains[order[-1]])
     for copy in sent:
         copy.wait_send()

time: 47.2 us -> 49.1 us (1.040)
  Pallas kernels: 45.8 us -> 47.6 us
    pallas_call x1, Pallas kernels: 43.9 us -> 45.7 us  [per_device(): pl.pallas_call(functools.partial(kernel, (n_hour, n_lat, n_lon, rows, col...]
where the time goes in v7:
time: 49.1 us; the launch traced here: 48.9 us
  Pallas kernels  47.6 us (97%)
  between operations  1.28 us (3%)
    pallas_call x1, Pallas kernels, per_device(): pl.pallas_call(functools.partial(kernel, (n_hour, n_lat, n_lon, rows, col...  45.7 us
    pallas_call x1, Pallas kernels, per_device(): pl.pallas_call(functools.partial(write_out, (at, n)), out_shape=(out, out...  1.89 us

profile of v7, /device:TPU:0, one launch (start us, length us, event | category | flops | bytes accessed | tf_op | source)
XLA Modules:
  0.0 48.9 jit_solution(11611106802720341124)
XLA Ops:
  1.3 45.7 %shard_map.59 = (f32[1,512,512]{2,1,0:T(8,128)S(1)}, f32[1,512,512]{2,1,0:T(8,128)S(1)}, f32[544,640]{1,0:T(8,128)S(1)}, f32[544,640]{1,0:T(8,128)S(1)}, f32[544...) custom-call(f32[1,512,512]{2,1,0:T(8,128)} %p_hbm.1, ...), custom_call_target="tpu_custom_call" | custom-call | tf_op jit(solution)/shard_map/pallas_call | solution.py:406
  47.0 1.9 %shard_map.60 = (f32[1,512,512]{2,1,0:T(8,128)}, f32[1,512,512]{2,1,0:T(8,128)}) custom-call(f32[1,512,512]{2,1,0:T(8,128)S(1)} %get-tuple-element.12.p_ref, f32[1,512,512]{2,1,0:T(8,128)S(1)} %get-tuple-element.13.s_ref, f32[544,640]{1,0:T(8,128)S(1)} %get-tuple-element.14.ds, f32[544,640]{1,0:T(8,128)S(1)} %get-tuple-element.15.first, ...), custom_call_target="tpu_custom_call" | custom-call | tf_op jit(solution)/shard_map/pallas_call | solution.py:423
